TPU v7x, 256 devices: a whole 4x4x8 slice. The times are simulated.
256 devices in a mesh: dp: 8 (over x_hi, y), patch: 32 (over x_lo, z, core).
Axes of the slice: x: 4 (x_hi: 2, x_lo: 2; x = x_hi * 2 + x_lo), y: 4, z: 8, core: 2. Of those that a mesh axis runs over, the one named last changes fastest.
Arguments:
- latent: bfloat16 [8, 64, 64, 640], P('dp', 'patch'), may hold values from -6 to 6
- cotangent: bfloat16 [8, 64, 64, 640], P('dp', 'patch'), may hold values from -6 to 6
- conv_weight: bfloat16 [3, 3, 640, 640], replicated, may hold values from -0.078125 to 0.078125
- query_weight: bfloat16 [640, 320], replicated, may hold values from -0.25 to 0.25
- key_weight: bfloat16 [640, 320], replicated, may hold values from -0.25 to 0.25
- value_weight: bfloat16 [640, 320], replicated, may hold values from -0.25 to 0.25
- out_weight: bfloat16 [320, 640], replicated, may hold values from -0.3125 to 0.3125
Outputs:
- grad_latent: bfloat16 [8, 64, 64, 640], P('dp', 'patch')
- grad_conv: float32 [3, 3, 640, 640], P(None, None, 'patch')
- grad_query: float32 [640, 320], replicated
- grad_key: float32 [640, 320], replicated
- grad_value: float32 [640, 320], replicated
- grad_out: float32 [320, 640], replicated
All inputs are finite; a program needn't handle non-finite values.
Results may differ from a plain program's by a relative error of at most 0.018.
Values may be sent and summed in bfloat16 or wider, within the bound.
A program may use at most 128 MiB of HBM per device.

v0:
```python
import jax
import jax.numpy as jnp
from jax import lax
from jax.sharding import PartitionSpec as P

NH = 5
HD = 64
AW = 320


def with_halo(value, sides, width):
    for axis, dim in sides:
        devices, length = (lax.axis_size(axis), value.shape[dim])
        up = [(i, (i + 1) % devices) for i in range(devices - 1)]
        down = [(j, i) for i, j in up]
        last = lax.slice_in_dim(value, length - width, length, axis=dim)
        leading = lax.slice_in_dim(value, 0, width, axis=dim)
        before = lax.ppermute(last, axis, up)
        after = lax.ppermute(leading, axis, down)
        value = jnp.concatenate([before, value, after], axis=dim)
    return value


def conv_rows(padded, weight, rows, cols, backward):
    total = jnp.zeros((rows * cols, weight.shape[3]), jnp.float32)
    for first in range(3):
        for second in range(3):
            window = padded[first : first + rows, second : second + cols].reshape(rows * cols, -1)
            if backward:
                tap = weight[2 - first, 2 - second]
                dims = (((1,), (1,)), ((), ()))
            else:
                tap = weight[first, second]
                dims = (((1,), (0,)), ((), ()))
            total = total + lax.dot_general(window, tap, dims, preferred_element_type=jnp.float32)
    return total


def outer_sum(left, right):
    return lax.dot_general(
        left, right, (((0,), (0,)), ((), ())), preferred_element_type=jnp.float32
    )


def pad_columns(field):
    return jnp.pad(field, ((0, 0), (1, 1), (0, 0)))


def body(latent, cotangent, conv_weight, query_weight, key_weight, value_weight, out_weight):
    rows, cols, chans = (latent.shape[1], latent.shape[2], latent.shape[3])
    count = rows * cols
    scale = HD ** (-0.5)
    padded = pad_columns(with_halo(latent[0], (("patch", 0),), 1))
    hidden = conv_rows(padded, conv_weight, rows, cols, False).astype(jnp.bfloat16)
    query = jnp.dot(hidden, query_weight, preferred_element_type=jnp.float32).astype(jnp.bfloat16)
    key = jnp.dot(hidden, key_weight, preferred_element_type=jnp.float32).astype(jnp.bfloat16)
    value = jnp.dot(hidden, value_weight, preferred_element_type=jnp.float32).astype(jnp.bfloat16)
    whole_key, whole_value = (
        lax.all_gather(key, "patch", axis=0, tiled=True),
        lax.all_gather(value, "patch", axis=0, tiled=True),
    )
    total = whole_key.shape[0]
    qh = query.reshape(count, NH, HD)
    kh_all = whole_key.reshape(total, NH, HD)
    vh_all = whole_value.reshape(total, NH, HD)
    scores = jnp.einsum("qhd,khd->hqk", qh, kh_all, preferred_element_type=jnp.float32) * scale
    top = jnp.max(scores, axis=2, keepdims=True)
    lse = top + jnp.log(jnp.sum(jnp.exp(scores - top), axis=2, keepdims=True))
    probs = jnp.exp(scores - lse)
    probs_b = probs.astype(jnp.bfloat16)
    attended = jnp.einsum("hqk,khd->qhd", probs_b, vh_all, preferred_element_type=jnp.float32)
    attended_b = attended.reshape(count, AW).astype(jnp.bfloat16)
    grad_flat = cotangent[0].reshape(count, chans)
    grad_att = lax.dot_general(
        grad_flat, out_weight, (((1,), (1,)), ((), ())), preferred_element_type=jnp.float32
    ).astype(jnp.bfloat16)
    grad_out = outer_sum(attended_b, grad_flat)
    gh = grad_att.reshape(count, NH, HD)
    delta = jnp.sum(gh.astype(jnp.float32) * attended, axis=2).T
    grad_probs = jnp.einsum("qhd,khd->hqk", gh, vh_all, preferred_element_type=jnp.float32)
    grad_scores_b = (probs * (grad_probs - delta[:, :, None])).astype(jnp.bfloat16)
    grad_q = (
        (
            jnp.einsum("hqk,khd->qhd", grad_scores_b, kh_all, preferred_element_type=jnp.float32)
            * scale
        )
        .reshape(count, AW)
        .astype(jnp.bfloat16)
    )
    own_key = key.reshape(count, NH, HD)
    own_value = value.reshape(count, NH, HD)
    whole_lse, whole_delta = (
        lax.all_gather(lse[:, :, 0].T, "patch", axis=0, tiled=True),
        lax.all_gather(delta.T, "patch", axis=0, tiled=True),
    )
    piece_query = lax.all_gather(query, "patch", axis=0, tiled=True)
    piece_grad = lax.all_gather(grad_att, "patch", axis=0, tiled=True)
    width = piece_query.shape[0]
    pq = piece_query.reshape(width, NH, HD)
    pg = piece_grad.reshape(width, NH, HD)
    local_scores = (
        jnp.einsum("qhd,khd->hqk", pq, own_key, preferred_element_type=jnp.float32) * scale
    )
    local_probs = jnp.exp(local_scores - whole_lse.T[:, :, None])
    local_grad = jnp.einsum("qhd,khd->hqk", pg, own_value, preferred_element_type=jnp.float32)
    local_scores_b = (local_probs * (local_grad - whole_delta.T[:, :, None])).astype(jnp.bfloat16)
    next_key = (
        jnp.einsum("hqk,qhd->khd", local_scores_b, pq, preferred_element_type=jnp.float32) * scale
    )
    next_value = jnp.einsum(
        "hqk,qhd->khd", local_probs.astype(jnp.bfloat16), pg, preferred_element_type=jnp.float32
    )
    grad_k = next_key.reshape(count, AW).astype(jnp.bfloat16)
    grad_v = next_value.reshape(count, AW).astype(jnp.bfloat16)
    grad_query, grad_key, grad_value, grad_out = lax.psum(
        (outer_sum(hidden, grad_q), outer_sum(hidden, grad_k), outer_sum(hidden, grad_v), grad_out),
        ("dp", "patch"),
    )
    back = (((1,), (1,)), ((), ()))
    grad_hidden = grad_flat.astype(jnp.float32)
    grad_hidden = grad_hidden + lax.dot_general(
        grad_q, query_weight, back, preferred_element_type=jnp.float32
    )
    grad_hidden = grad_hidden + lax.dot_general(
        grad_k, key_weight, back, preferred_element_type=jnp.float32
    )
    grad_hidden = grad_hidden + lax.dot_general(
        grad_v, value_weight, back, preferred_element_type=jnp.float32
    )
    grad_hidden = grad_hidden.astype(jnp.bfloat16)
    grad_pad = pad_columns(with_halo(grad_hidden.reshape(rows, cols, chans), (("patch", 0),), 1))
    grad_latent = (
        conv_rows(grad_pad, conv_weight, rows, cols, True)
        .reshape(1, rows, cols, chans)
        .astype(jnp.bfloat16)
    )
    channel_share = lax.all_to_all(latent[0], "patch", split_axis=2, concat_axis=0, tiled=True)
    share_pad = jnp.pad(channel_share, ((1, 1), (1, 1), (0, 0)))
    share_width = channel_share.shape[2]
    piece = lax.all_gather(grad_hidden.reshape(rows, cols, chans), "patch", axis=0, tiled=True)
    piece_rows = piece.shape[0]
    flat_grad = piece.reshape(piece_rows * cols, chans)
    terms = []
    for first in range(3):
        band = lax.dynamic_slice_in_dim(share_pad, first, piece_rows, 0)
        for second in range(3):
            window = band[:, second : second + cols].reshape(piece_rows * cols, share_width)
            terms.append(outer_sum(window, flat_grad))
    own_taps = jnp.stack(terms).reshape(3, 3, share_width, chans)
    grad_conv = lax.psum(own_taps.astype(jnp.bfloat16), "dp").astype(jnp.float32)
    return (grad_latent, grad_conv, grad_query, grad_key, grad_value, grad_out)


def solution(mesh):
    placed = (P("dp", "patch", None, None), P("dp", "patch", None, None), P(), P(), P(), P(), P())
    return jax.shard_map(
        body,
        mesh=mesh,
        in_specs=placed,
        out_specs=(P("dp", "patch", None, None), P(None, None, "patch", None), P(), P(), P(), P()),
        check_vma=False,
    )
```

profile of v0, /device:TPU:8, one launch (start us, length us, event | category | flops | bytes accessed | tf_op | source)
XLA Modules:
  0.0 785.6 jit_solution(5522777074956671610)
XLA Ops:
  9.9 3.0 collective-permute-start
  26.5 70.8 %all-gather.6.cloned.1.call-done = bf16[4096,320]{0,1:T(8,128)(2,1)} async-done(((bf16[128,320]{0,1:T(8,128)(2,1)}), bf16[4096,320]{0,1:T(8,128)(2,1)}) %all-gather.6.cloned.1.call-update) | async-done | bytes 2621456 | tf_op jit(solution)/shard_map/all_gather | solution.py:59
  97.3 3.4 multiply_reduce_fusion
  100.8 4.0 copy-done.2
  104.8 1.8 exponential_reduce_fusion
  106.6 59.2 %all-gather.8.cloned.1.call-done = bf16[4096,320]{0,1:T(8,128)(2,1)} async-done(((bf16[128,320]{0,1:T(8,128)(2,1)}), bf16[4096,320]{0,1:T(8,128)(2,1)}) %all-gather.8.cloned.1.call-update) | async-done | bytes 2621456 | tf_op jit(solution)/shard_map/all_gather | solution.py:60
  165.8 7.4 fusion.130
  173.3 35.5 %all_gather.26 = f32[4096,5]{0,1:T(8,128)} all-gather(f32[128,5]{0,1:T(8,128)S(1)} %get-tuple-element.23), channel_id=1, replica_groups=mesh['dp'=8,'patch'=32] {'patch'}, dimensions={0}, use_global_device_ids=true | all-gather | bytes 84480 | tf_op jit(solution)/shard_map/all_gather | solution.py:94
  208.8 31.2 %all_gather.24 = f32[4096,5]{0,1:T(8,128)S(1)} all-gather(f32[128,5]{0,1:T(8,128)S(1)} %bitcast.341), channel_id=1, replica_groups=mesh['dp'=8,'patch'=32] {'patch'}, dimensions={0}, use_global_device_ids=true | all-gather | bytes 84480 | tf_op jit(solution)/shard_map/all_gather | solution.py:93
  240.0 9.6 %fusion.22 = bf16[5,64,128]{2,1,0:T(8,128)(2,1)} fusion(bf16[4096,5,64]{0,2,1:T(8,128)(2,1)S(1)} %bitcast.289, f32[5,128,4096]{2,1,0:T(8,128)} %copy-done.2, bf16[128,5,64]{0,2,1:T(8,128)(2,1)} %bitcast.314, bf16[4096,5,64]{0,2,1:T(8,128)(2,1)} %bitcast.304, f32[5,128]{1,0:T(8,128)S(1)} %bitcast.342, f32[5,128]{1,0:T(8,128)S(1)} %log_add_fusion), kind=kOutput, calls=%fused_computation.41 | convolution fusion | flops 684277760 | bytes 15897600 | tf_op jit(solution)/shard_map/hqk,khd->qhd/dot_general | solution.py:84
  249.6 2.0 convolution_add_fusion.2
  251.6 7.6 fusion.131
  259.2 44.1 %all-gather.12.cloned.1.call-done = bf16[4096,320]{0,1:T(8,128)(2,1)} async-done(((bf16[128,320]{0,1:T(8,128)(2,1)}), bf16[4096,320]{0,1:T(8,128)(2,1)}) %all-gather.12.cloned.1.call-update) | async-done | bytes 2621456 | tf_op jit(solution)/shard_map/all_gather | solution.py:97
  303.3 7.7 fusion.24
  311.1 12.6 %fusion.23 = bf16[5,64,128]{2,1,0:T(8,128)(2,1)} fusion(bf16[4096,5,64]{0,2,1:T(8,128)(2,1)} %bitcast.302, f32[5,4096,128]{2,1,0:T(8,128)} %fusion.131, bf16[4096,5,64]{0,2,1:T(8,128)(2,1)S(1)} %bitcast.298, bf16[128,5,64]{0,2,1:T(8,128)(2,1)} %bitcast.338, f32[5,4096]{1,0:T(8,128)} %bitcast.340, f32[5,4096]{1,0:T(8,128)S(1)} %bitcast.300), kind=kOutput, calls=%fused_computation.42 | convolution fusion | flops 684277760 | bytes 16056320 | tf_op jit(solution)/shard_map/hqk,qhd->khd/dot_general | solution.py:108
  325.0 2.0 fusion.14
  327.5 15.9 %all_to_all.18 = bf16[32,2,1280]{2,1,0:T(2,128)(2,1)S(1)} all-to-all(bf16[32,2,1280]{2,1,0:T(2,128)(2,1)S(1)} %reshape.179), channel_id=1, replica_groups=mesh['dp'=8,'patch'=32] {'patch'}, dimensions={0} | all-to-all | bytes 327680 | tf_op jit(solution)/shard_map/all_to_all | solution.py:137
  346.0 3.3 collective-permute-start.2
  349.3 2.0 fusion.133
  351.3 2.0 fusion.134
  353.3 2.0 fusion.135
  355.4 39.1 %all-gather.14.cloned.1.call-done = bf16[64,64,640]{2,1,0:T(8,128)(2,1)} async-done(((bf16[2,64,640]{2,1,0:T(8,128)(2,1)}), bf16[64,64,640]{2,1,0:T(8,128)(2,1)}) %all-gather.14.cloned.1.call-update) | async-done | bytes 5242896 | tf_op jit(solution)/shard_map/all_gather | solution.py:140
  394.5 3.7 fusion.53
  398.2 3.4 fusion.51
  423.2 2.2 fusion.15
  425.4 69.9 %all-reduce.7.cloned.1.call-done = bf16[3,3,20,640]{3,2,1,0:T(8,128)(2,1)} async-done(((bf16[3,3,20,640]{3,2,1,0:T(8,128)(2,1)}), bf16[3,3,20,640]{3,2,1,0:T(8,128)(2,1)}) %all-reduce.7.cloned.1.call-update) | async-done | bytes 230416 | tf_op jit(solution)/shard_map/psum | solution.py:150
  495.3 1.8 convert_element_type.119
  497.1 273.3 %all-reduce.9.cloned.1.call-done = (f32[640,320]{0,1:T(8,128)}, f32[640,320]{0,1:T(8,128)}, f32[640,320]{0,1:T(8,128)}, f32[320,640]{1,0:T(8,128)}) async-done(((f32[640,320]{0,1:T(8,128)}, f32[640,320]{0,1:T(8,128)}, f32[640,320]{0,1:T(8,128)}, f32[320,640]{1,0:T(8,128)}), (f32[640,320]{0,1:T(8,128)}, f32[640,320]{0,1:T(8,128)}, f32[640,320]{0,1:T(8,128)}, ...) | async-done | bytes 3276816 | tf_op jit(solution)/shard_map/psum | solution.py:115
  770.4 2.1 copy.35
  772.5 2.1 copy.36
  774.6 2.1 copy.37
  776.7 2.1 copy.38
  (102 shorter events, 41.7 us)
Async XLA Ops:
  7.2 17.3 %copy-start = (bf16[640,320]{0,1:T(8,128)(2,1)S(1)}, bf16[640,320]{0,1:T(8,128)(2,1)}, u32[]{:S(2)}) copy-start(bf16[640,320]{0,1:T(8,128)(2,1)} %param.10) | copy-start | bytes 1228804
  7.2 14.0 %copy-start.6 = (bf16[1,2,64,640]{3,2,1,0:T(8,128)(2,1)S(1)}, bf16[1,2,64,640]{3,2,1,0:T(8,128)(2,1)}, u32[]{:S(2)}) copy-start(bf16[1,2,64,640]{3,2,1,0:T(8,128)(2,1)} %param.7) | copy-start | bytes 491524
  7.2 90.1 %all-gather.6.cloned.1.call-start = ((), (), s32[]{:S(2)}) async-start(), calls=%async_computation.1 | async-start | bytes 2703360 | tf_op jit(solution)/shard_map/all_gather | solution.py:59
  7.2 13.3 %copy-start.3 = (bf16[3,3,640,640]{3,2,1,0:T(8,128)(2,1)S(1)}, bf16[3,3,640,640]{3,2,1,0:T(8,128)(2,1)}, u32[]{:S(2)}) copy-start(bf16[3,3,640,640]{3,2,1,0:T(8,128)(2,1)} %param.9) | copy-start | bytes 22118404
  8.4 4.6 collective-permute-start.1
  9.9 3.9 collective-permute-start
  15.0 7.5 copy-start.8
  16.5 7.0 copy-start.10
  18.0 7.5 copy-start.11
  18.1 7.4 copy-start.14
  23.4 142.4 %all-gather.8.cloned.1.call-start = ((), (), s32[]{:S(2)}) async-start(), calls=%async_computation.2 | async-start | bytes 2703360 | tf_op jit(solution)/shard_map/all_gather | solution.py:60
  24.4 227.2 %all-gather.10.cloned.1.call-start = ((), (), s32[]{:S(2)}) async-start(), calls=%async_computation.3 | async-start | bytes 2703360 | tf_op jit(solution)/shard_map/all_gather | solution.py:96
  25.4 277.9 %all-gather.12.cloned.1.call-start = ((), (), s32[]{:S(2)}) async-start(), calls=%async_computation.4 | async-start | bytes 2703360 | tf_op jit(solution)/shard_map/all_gather | solution.py:97
  26.4 368.1 %all-gather.14.cloned.1.call-start = ((), (), s32[]{:S(2)}) async-start(), calls=%async_computation.5 | async-start | bytes 5406720 | tf_op jit(solution)/shard_map/all_gather | solution.py:140
  100.7 4.0 copy-start.2
  100.8 65.1 %copy-start.13 = (bf16[128,320]{0,1:T(8,128)(2,1)S(1)}, bf16[128,320]{0,1:T(8,128)(2,1)}, u32[]{:S(2)}) copy-start(bf16[128,320]{0,1:T(8,128)(2,1)} %convolution_convert_fusion.1) | copy-start | bytes 245764
  106.6 133.4 %copy-start.4 = (bf16[4096,320]{0,1:T(8,128)(2,1)S(1)}, bf16[4096,320]{0,1:T(8,128)(2,1)}, u32[]{:S(2)}) copy-start(bf16[4096,320]{0,1:T(8,128)(2,1)} %all-gather.6.cloned.1.call-done) | copy-start | bytes 7864324
  303.3 7.7 copy-start.7
  311.1 12.6 %copy-start.9 = (bf16[640,320]{0,1:T(8,128)(2,1)S(1)}, bf16[640,320]{0,1:T(8,128)(2,1)}, u32[]{:S(2)}) copy-start(bf16[640,320]{0,1:T(8,128)(2,1)} %param.11) | copy-start | bytes 1228804
  327.0 168.3 %all-reduce.7.cloned.1.call-start = ((), (), s32[]{:S(2)}) async-start(), calls=%async_computation.6 | async-start | bytes 552960 | tf_op jit(solution)/shard_map/psum | solution.py:150
  344.7 66.1 %collective-permute-start.3 = (bf16[1,64,640]{2,1,0:T(8,128)(2,1)S(1)}, bf16[1,64,640]{2,1,0:T(8,128)(2,1)S(1)}, u32[]{:S(2)}, u32[]{:S(2)}) collective-permute-start(bf16[1,64,640]{2,1,0:T(8,128)(2,1)S(1)} %get-tuple-element.27), channel_id=1, source_target_pairs={{1,0},{2,1},{3,2},{4,3},{5,4},{6,5},{7,6},{8,7},{9,8},{10,9},{11,1... | collective-permute-start | bytes 245768 | tf_op jit(solution)/shard_map/ppermute | solution.py:19
  346.0 64.8 %collective-permute-start.2 = (bf16[1,64,640]{2,1,0:T(8,128)(2,1)S(1)}, bf16[1,64,640]{2,1,0:T(8,128)(2,1)S(1)}, u32[]{:S(2)}, u32[]{:S(2)}) collective-permute-start(bf16[1,64,640]{2,1,0:T(8,128)(2,1)S(1)} %get-tuple-element.26), channel_id=1, source_target_pairs={{0,1},{1,2},{2,3},{3,4},{4,5},{5,6},{6,7},{7,8},{8,9},{9,10},{10,1... | collective-permute-start | bytes 245768 | tf_op jit(solution)/shard_map/ppermute | solution.py:18
  394.5 7.1 slice-start
  394.5 7.1 slice-start.1
  405.7 3.9 copy-start.12
  405.7 3.9 copy-start.16
  406.7 4.0 copy-start.5
  408.7 0.7 copy-start.15
  409.5 360.9 %all-reduce.9.cloned.1.call-start = ((), (), s32[]{:S(2)}) async-start(), calls=%async_computation.7 | async-start | bytes 6553600 | tf_op jit(solution)/shard_map/psum | solution.py:115
  417.1 361.6 %copy-start.1 = (bf16[640,320]{0,1:T(8,128)(2,1)S(1)}, bf16[640,320]{0,1:T(8,128)(2,1)}, u32[]{:S(2)}) copy-start(bf16[640,320]{0,1:T(8,128)(2,1)} %param.10) | copy-start | bytes 1228804
Sparse Core Ops, SparseCore 0:
  23.6 73.7 all-gather.5
  99.7 66.1 all-gather.7
  168.2 66.6 all-gather.9
  237.0 66.2 all-gather.11
  327.2 67.2 all-gather.13
  409.6 85.6 all-reduce.6
  503.0 267.3 all-reduce.8
where the time goes:
time: 787 us; the launch traced here: 786 us
  waiting for transfers between devices  557 us (71%)
  matrix products  99.4 us (13%)
  blocking collectives  82.6 us (10%)
  local copies, waits for them, and re-layouts  16.2 us (2%)
  between operations  14.7 us (2%)
  starting transfers between devices  9.46 us (1%)
    psum x1, waiting for transfers between devices, body(): lax.psum((outer_sum(hidden, grad_q), outer_sum(hidden, grad_k), outer_sum...  273 us
    all_gather x1, waiting for transfers between devices, body(): lax.all_gather(key, 'patch', axis=0, tiled=True)  70.8 us
    psum x1, waiting for transfers between devices, body(): lax.psum(own_taps.astype(jnp.bfloat16), 'dp').astype(jnp.float32)  69.9 us
    all_gather x1, waiting for transfers between devices, body(): lax.all_gather(value, 'patch', axis=0, tiled=True)  59.2 us
    all_gather x1, waiting for transfers between devices, body(): piece_grad = lax.all_gather(grad_att, 'patch', axis=0, tiled=True)  44.1 us
    all_gather x1, waiting for transfers between devices, body(): lax.all_gather(grad_hidden.reshape(rows, cols, chans), 'patch', axis=0, t...  39.1 us
    all_gather x1, blocking collectives, body(): lax.all_gather(delta.T, 'patch', axis=0, tiled=True)  35.5 us
    all_gather x1, blocking collectives, body(): lax.all_gather(lse[:, :, 0].T, 'patch', axis=0, tiled=True)  31.2 us
  transfers between devices with their start and end apart: 11, of which 7 were waited for; matrix products, arithmetic and copies ran while one was open for 9% of the time, Pallas kernels for 0%

commit v1 on v0

v1 whole, which is shorter than its diff:
```python
import functools
import jax
import jax.numpy as jnp
from jax import lax
from jax.experimental import pallas as pl
from jax.experimental.pallas import tpu as pltpu
from jax.sharding import PartitionSpec as P

NH = 5
HD = 64
AW = 320
MESH = pl.DeviceIdType.MESH
F32 = jnp.float32
BF16 = jnp.bfloat16


def place():
    p = lax.axis_index("patch")
    return lax.axis_index("dp"), p // 16, lax.rem(p, 16) // 2, lax.rem(p, 2)


def send(src, dst, send_sem, recv_sem, device):
    copy = pltpu.make_async_remote_copy(
        src_ref=src, dst_ref=dst, send_sem=send_sem, recv_sem=recv_sem,
        device_id=device, device_id_type=MESH,
    )
    copy.start()
    return copy


def greet(devices):
    barrier = pltpu.get_barrier_semaphore()
    for device in devices:
        pl.semaphore_signal(barrier, inc=1, device_id=device, device_id_type=MESH)
    pl.semaphore_wait(barrier, len(devices))


NT = (((1,), (1,)), ((), ()))
LOG2E = 1.4426950408889634


def remote(src, dst, send_sem, recv_sem, device):
    return pltpu.make_async_remote_copy(
        src_ref=src, dst_ref=dst, send_sem=send_sem, recv_sem=recv_sem,
        device_id=device, device_id_type=MESH,
    )


def attend_kernel(x_ref, out_ref, kv, qd, qs, gs, qt, gt, scores, slope, pb, sb, top, low, att, delta, dq,
                  part, box_up, box_down, ahead, behind, stage, res, kv_s, kv_r, qd_s, qd_r, up_s, up_r, down_s, down_r,
                  rup_s, rup_r, rdown_s, rdown_r, o_s, o_r, g_s, g_r):
    dp, xlo, z, core = place()
    j = xlo * 2 + core

    def at_z(step):
        return (dp, xlo * 16 + lax.rem(z + step + 8, 8) * 2 + core)

    def in_quad(step):
        m = lax.rem(j + step, 4)
        return m, (dp, (m // 2) * 16 + z * 2 + lax.rem(m, 2))

    def rows(m):
        return pl.ds(pl.multiple_of(m * 128, 128), 128)

    greet([at_z(1), at_z(-1)] + [in_quad(s)[1] for s in range(1, 4)])

    first, second = [], []
    for s in range(1, 4):
        m, device = in_quad(s)
        first.append(send(x_ref.at[m, 0:2], kv.at[z, :, rows(j), :], kv_s.at[s], kv_r.at[s], device))
    for s in range(1, 4):
        m, device = in_quad(s)
        second.append(send(x_ref.at[m, 2:4], qd.at[:, rows(j), :], qd_s.at[s], qd_r.at[s], device))
    for t in range(2):
        kv[z, t, rows(j), :] = x_ref[j, t]
        qd[t, rows(j), :] = x_ref[j, 2 + t]
    lane = lax.broadcasted_iota(jnp.int32, (128, 128), 1)
    left = lane < 64
    own = x_ref[j, 2:4].astype(F32)
    qs[512:640] = jnp.where(left, 0.0, own[0]).astype(BF16)
    gs[512:640] = jnp.where(left, 0.0, own[1]).astype(BF16)
    top[...] = jnp.full(top.shape, -jnp.inf, F32)
    low[...] = jnp.zeros(low.shape, F32)
    att[...] = jnp.zeros(att.shape, F32)
    dq[...] = jnp.zeros(dq.shape, F32)

    def ring_up(s):
        k = lax.rem(z + 8 - s, 8)
        return remote(kv.at[k], kv.at[k], up_s.at[s], up_r.at[s], at_z(1))

    def ring_down(s):
        k = lax.rem(z + s, 8)
        return remote(kv.at[k], kv.at[k], down_s.at[s], down_r.at[s], at_z(-1))

    for copy in first:
        copy.wait()
    ring_up(0).start()
    ring_down(0).start()
    for copy in second:
        copy.wait()
    for m in range(4):
        pair = qd[:, m * 128 : m * 128 + 128, :].astype(F32)
        qs[m * 128 : m * 128 + 128] = jnp.where(left, pair[0], 0.0).astype(BF16)
        gs[m * 128 : m * 128 + 128] = jnp.where(left, pair[1], 0.0).astype(BF16)
    qt[...] = qs[...].astype(F32).T.astype(BF16)
    gt[...] = gs[...].astype(F32).T.astype(BF16)

    def pass_one(t, carry):
        for s in range(4):
            @pl.when(t == 2 * s + 1)
            def _():
                ring_up(s).wait_recv()
                if s < 3:
                    ring_up(s + 1).start()

            if s < 3:
                @pl.when(t == 2 * s + 2)
                def _():
                    ring_down(s).wait_recv()
                    if s < 2:
                        ring_down(s + 1).start()

        offset = jnp.where(lax.rem(t, 2) == 1, 8 - (t + 1) // 2, t // 2)
        b = lax.rem(z + offset, 8)
        scores[b] = lax.dot_general(qs[...], kv[b, 0], NT, preferred_element_type=F32) * LOG2E
        for i in range(5):
            r = slice(128 * i, 128 * i + 128)
            s = scores[b, r]
            old = top[r]
            new = jnp.maximum(old, jnp.max(s, axis=1, keepdims=True))
            p = jnp.exp2(s - new)
            fade = jnp.exp2(old - new)
            low[r] = low[r] * fade + jnp.sum(p, axis=1, keepdims=True)
            top[r] = new
            att[r] = att[r] * fade
            pb[r] = p.astype(BF16)
        att[...] += jnp.dot(pb[...], kv[b, 1], preferred_element_type=F32)
        return carry

    lax.fori_loop(0, 8, pass_one, 0)
    for i in range(5):
        r = slice(128 * i, 128 * i + 128)
        value = att[r] / low[r]
        top[r] = top[r] + jnp.log2(low[r])
        att[r] = value
        delta[r] = jnp.sum(value * gs[r].astype(F32), axis=1, keepdims=True)
    stage[0] = att[0:512].astype(BF16)
    early = []
    for s in range(1, 4):
        m, device = in_quad(s)
        early.append(send(stage.at[0, rows(m), :], res.at[j, 0], o_s.at[s], o_r.at[s], device))

    def sum_up(s):
        return remote(box_up.at[s], ahead.at[s], rup_s.at[s], rup_r.at[s], at_z(1))

    def sum_down(s):
        return remote(
            box_down.at[s], behind.at[s], rdown_s.at[s], rdown_r.at[s], at_z(-1),
        )

    def pass_two(t, carry):
        offset = jnp.where(lax.rem(t, 2) == 0, 4 + t // 2, 4 - (t + 1) // 2)
        b = lax.rem(z + offset, 8)
        slope[...] = lax.dot_general(gs[...], kv[b, 1], NT, preferred_element_type=F32)
        for i in range(5):
            r = slice(128 * i, 128 * i + 128)
            p = jnp.exp2(scores[b, r] - top[r])
            pb[r] = p.astype(BF16)
            sb[r] = (p * (slope[r] - delta[r])).astype(BF16)
        dq[...] += jnp.dot(sb[...], kv[b, 0], preferred_element_type=F32)
        part[0] = jnp.dot(qt[...], sb[...], preferred_element_type=F32)
        part[1] = jnp.dot(gt[...], pb[...], preferred_element_type=F32)

        @pl.when(t == 0)
        def _():
            box_up[0] = part[...].astype(BF16)
            sum_up(0).start()

        @pl.when(t == 2)
        def _():
            box_down[0] = part[...].astype(BF16)
            sum_down(0).start()

        for s in range(3):
            @pl.when(t == 2 * s + 1)
            def _():
                sum_up(s).wait_recv()
                box_up[s + 1] = (part[...] + ahead[s].astype(F32)).astype(BF16)
                sum_up(s + 1).start()

        for s in range(2):
            @pl.when(t == 2 * s + 4)
            def _():
                sum_down(s).wait_recv()
                box_down[s + 1] = (part[...] + behind[s].astype(F32)).astype(BF16)
                sum_down(s + 1).start()

        return carry

    lax.fori_loop(0, 8, pass_two, 0)
    stage[1] = (dq[0:512] * HD ** -0.5).astype(BF16)
    sum_up(3).wait_recv()
    sum_down(2).wait_recv()
    for t in range(2):
        whole = part[t] + ahead[3, t].astype(F32) + behind[2, t].astype(F32)
        stage[2 + t] = whole.T.astype(BF16)
    late = []
    for s in range(1, 4):
        m, device = in_quad(s)
        late.append(send(stage.at[1:4, rows(m), :], res.at[j, 1:4], g_s.at[s], g_r.at[s], device))
    for t in range(4):
        res[j, t] = stage[t, rows(j), :]
    for s in range(4):
        ring_up(s).wait_send()
        sum_up(s).wait_send()
    for s in range(3):
        ring_down(s).wait_send()
        sum_down(s).wait_send()
    for copy in early + late:
        copy.wait()

    def swap(a):
        return pltpu.roll(a, 64, axis=1)

    last = [att[512:640], dq[512:640] * HD ** -0.5]
    for t in range(2, 4):
        last.append(sum(res[m, t].astype(F32) for m in range(4)))
    for t in range(4):
        for i in range(2):
            pair = jnp.where(left, res[2 * i, t].astype(F32), swap(res[2 * i + 1, t].astype(F32)))
            out_ref[t, :, 128 * i : 128 * i + 128] = pair.astype(BF16)
        out_ref[t, :, 256:384] = jnp.where(left, swap(last[t]), 0.0).astype(BF16)


def attend(x):
    dma = pltpu.SemaphoreType.DMA
    vmem = pl.BlockSpec(memory_space=pltpu.VMEM)
    return pl.pallas_call(
        attend_kernel,
        out_shape=jax.ShapeDtypeStruct((4, 128, 384), BF16),
        in_specs=[vmem],
        out_specs=vmem,
        scratch_shapes=[
            pltpu.VMEM((8, 2, 512, 128), BF16),
            pltpu.VMEM((2, 512, 128), BF16),
            pltpu.VMEM((640, 128), BF16),
            pltpu.VMEM((640, 128), BF16),
            pltpu.VMEM((128, 640), BF16),
            pltpu.VMEM((128, 640), BF16),
            pltpu.VMEM((8, 640, 512), F32),
            pltpu.VMEM((640, 512), F32),
            pltpu.VMEM((640, 512), BF16),
            pltpu.VMEM((640, 512), BF16),
            pltpu.VMEM((640, 1), F32),
            pltpu.VMEM((640, 1), F32),
            pltpu.VMEM((640, 128), F32),
            pltpu.VMEM((640, 1), F32),
            pltpu.VMEM((640, 128), F32),
            pltpu.VMEM((2, 128, 512), F32),
            pltpu.VMEM((4, 2, 128, 512), BF16),
            pltpu.VMEM((3, 2, 128, 512), BF16),
            pltpu.VMEM((4, 2, 128, 512), BF16),
            pltpu.VMEM((3, 2, 128, 512), BF16),
            pltpu.VMEM((4, 512, 128), BF16),
            pltpu.VMEM((4, 4, 128, 128), BF16),
            dma((4,)), dma((4,)), dma((4,)), dma((4,)),
            dma((4,)), dma((4,)), dma((3,)), dma((3,)),
            dma((4,)), dma((4,)), dma((3,)), dma((3,)),
            dma((4,)), dma((4,)), dma((4,)), dma((4,)),
        ],
        compiler_params=pltpu.CompilerParams(
            collective_id=1, has_side_effects=True, vmem_limit_bytes=48 * 1024 * 1024
        ),
        name="attend",
    )(x)


def shifted(rows, j):
    before = jnp.where(j == 0, 0.0, pltpu.roll(rows, 1, axis=0))
    after = jnp.where(j == 63, 0.0, pltpu.roll(rows, 63, axis=0))
    return before, rows, after


def first_kernel(lat_ref, cot_ref, wq_ref, wk_ref, wv_ref, wo_ref, w_ref, hid_ref, x_ref, lhs_ref,
                 w, w_sem, halo, turned, sbuf, share, sh, acc, tmp, halo_s, halo_r, share_s, share_r):
    dp = lax.axis_index("dp")
    p = lax.axis_index("patch")

    def at(step):
        other = lax.rem(p + step + 32, 32)
        return other, (dp, other)

    loads = []
    for t in range(9):
        copy = pltpu.make_async_copy(w_ref.at[t], w.at[t], w_sem.at[t])
        copy.start()
        loads.append(copy)
    barrier = pltpu.get_barrier_semaphore()

    def hello(s, carry):
        pl.semaphore_signal(barrier, inc=1, device_id=at(s)[1], device_id_type=MESH)
        return carry

    lax.fori_loop(1, 32, hello, 0)
    turned[0:640] = lat_ref[...].astype(F32).T
    turned[640:656] = jnp.zeros((16, 128), F32)
    for k in range(32):
        sbuf[k] = turned[20 * k : 20 * k + 32].astype(BF16)
    share[0] = jnp.zeros((32, 128), BF16)
    share[33] = jnp.zeros((32, 128), BF16)
    share[p + 1] = sbuf[p]
    pl.semaphore_wait(barrier, 31)
    near = [
        send(lat_ref.at[64:128], halo.at[0], halo_s.at[0], halo_r.at[0], at(1)[1]),
        send(lat_ref.at[0:64], halo.at[1], halo_s.at[1], halo_r.at[1], at(-1)[1]),
    ]

    def share_copy(s):
        other, device = at(s)
        return remote(sbuf.at[other], share.at[p + 1], share_s.at[s], share_r.at[s], device)

    def share_start(s, carry):
        share_copy(s).start()
        return carry

    lax.fori_loop(1, 32, share_start, 0)

    lane = lax.broadcasted_iota(jnp.int32, (128, 128), 1)
    left = lane < 64

    def pack(value, t):
        tmp[:, 0:320] = value.astype(BF16).astype(F32)
        low, mid = tmp[:, 0:128], tmp[:, 128:256]
        last = pltpu.roll(tmp[:, 256:384], 64, axis=1)
        heads = (low, pltpu.roll(low, 64, axis=1), mid, pltpu.roll(mid, 64, axis=1))
        for m in range(4):
            x_ref[m, t] = jnp.where(left, heads[m], last).astype(BF16)

    tmp[:, 256:384] = jnp.zeros((128, 128), F32)
    pack(lax.dot_general(cot_ref[...], wo_ref[...], NT, preferred_element_type=F32), 3)
    for copy in near:
        copy.wait()
    j = lax.broadcasted_iota(jnp.int32, (64, 640), 0)
    rows = (
        jnp.where(p > 0, halo[0].astype(F32), 0.0),
        lat_ref[0:64].astype(F32),
        lat_ref[64:128].astype(F32),
        jnp.where(p < 31, halo[1].astype(F32), 0.0),
    )
    for r in range(4):
        moved = shifted(rows[r], j)
        for b in range(3):
            sh[b, 64 * r : 64 * r + 64] = moved[b].astype(BF16)
    for t in range(9):
        a, b = t // 3, t % 3
        loads[t].wait()
        term = jnp.dot(sh[b, 64 * a : 64 * a + 128], w[t], preferred_element_type=F32)
        if t:
            acc[...] += term
        else:
            acc[...] = term
    hid_ref[...] = acc[...].astype(BF16)
    pack(jnp.dot(hid_ref[...], wk_ref[...], preferred_element_type=F32), 0)
    pack(jnp.dot(hid_ref[...], wv_ref[...], preferred_element_type=F32), 1)
    pack(jnp.dot(hid_ref[...], wq_ref[...], preferred_element_type=F32), 2)
    for m in range(4):
        x_ref[m, 2] = (x_ref[m, 2].astype(F32) * HD ** -0.5).astype(BF16)

    def share_end(s, carry):
        share_copy(s).wait()
        return carry

    lax.fori_loop(1, 32, share_end, 0)
    col = lax.broadcasted_iota(jnp.int32, (32, 128), 1)
    side = col < 64
    col = lax.rem(col, 64)

    def windows(q, carry):
        here = share[q + 1].astype(F32)
        turn = pltpu.roll(here, 64, axis=1)
        above = jnp.where(side, pltpu.roll(share[q].astype(F32), 64, axis=1), turn)
        below = jnp.where(side, turn, pltpu.roll(share[q + 2].astype(F32), 64, axis=1))
        place = pl.ds(pl.multiple_of(lax.rem(q, 2) * 128, 128), 128)
        for a, value in enumerate((above, here, below)):
            three = (
                jnp.where(col == 0, 0.0, pltpu.roll(value, 1, axis=1)),
                value,
                jnp.where(col == 63, 0.0, pltpu.roll(value, 127, axis=1)),
            )
            for b in range(3):
                t = 3 * a + b
                lhs_ref[q // 2, 32 * t : 32 * t + 32, place] = three[b].astype(BF16)
        return carry

    lax.fori_loop(0, 32, windows, 0)


def first(latent, cotangent, wq, wk, wv, wo, taps):
    dma = pltpu.SemaphoreType.DMA
    vmem = pl.BlockSpec(memory_space=pltpu.VMEM)
    return pl.pallas_call(
        first_kernel,
        out_shape=(
            jax.ShapeDtypeStruct((128, 640), BF16),
            jax.ShapeDtypeStruct((4, 4, 128, 128), BF16),
            jax.ShapeDtypeStruct((16, 288, 256), BF16),
        ),
        in_specs=[vmem] * 6 + [pl.BlockSpec(memory_space=pl.ANY)],
        out_specs=(vmem,) * 3,
        scratch_shapes=[
            pltpu.VMEM((9, 640, 640), BF16),
            dma((9,)),
            pltpu.VMEM((2, 64, 640), BF16),
            pltpu.VMEM((656, 128), F32),
            pltpu.VMEM((32, 32, 128), BF16),
            pltpu.VMEM((34, 32, 128), BF16),
            pltpu.VMEM((3, 256, 640), BF16),
            pltpu.VMEM((128, 640), F32),
            pltpu.VMEM((128, 384), F32),
            dma((2,)), dma((2,)), dma((32,)), dma((32,)),
        ],
        compiler_params=pltpu.CompilerParams(
            collective_id=2, has_side_effects=True, vmem_limit_bytes=48 * 1024 * 1024
        ),
        name="first",
    )(latent, cotangent, wq, wk, wv, wo, taps)


def finish_kernel(parts_ref, hid_ref, cot_ref, wq_ref, wk_ref, wv_ref, lhs_ref, w_ref, out_ref, taps_ref, lat_ref,
                  w, w_sem, gh, halo, sh, acc, prod, small, dqk, dva, dvb, turned, aturned, xs, half, ya, yb, yc, yd,
                  plane, xin, xsum, zin, zfull, pfull, ob, tb, tin, halo_s, halo_r, up_s, down_s, over_s, sib_s, own_r, sib_r,
                  pair_s, pair_r, y_s, y_r, x_s, x_r, z_s, z_r, zb_s, zb_r, xb_s, xb_r, yb_s, yb_r, fin_s, fin_r,
                  t_s, t_r, u_s, u_r):
    dp, xlo, z, core = place()
    p = lax.axis_index("patch")
    xhi, y = dp // 4, lax.rem(dp, 4)
    x = xhi * 2 + xlo
    sib = (dp, xlo * 16 + z * 2 + 1 - core)
    over = (dp, (1 - xlo) * 16 + z * 2 + core)

    def at_z(s):
        other = lax.rem(z + s + 8, 8)
        return other, (dp, xlo * 16 + other * 2 + core)

    def at_y(s):
        other = lax.rem(y + s + 4, 4)
        return other, (xhi * 4 + other, p)

    def at_x(s):
        other = lax.rem(x + s, 4)
        return other, (other // 2 * 4 + y, lax.rem(other, 2) * 16 + z * 2 + core)

    def at_dp(s):
        other = lax.rem(dp + s, 8)
        return other, (other, p)

    def at_p(s):
        return (dp, lax.rem(p + s + 32, 32))

    loads = []
    for t in range(9):
        copy = pltpu.make_async_copy(w_ref.at[t], w.at[t], w_sem.at[t])
        copy.start()
        loads.append(copy)
    greet(
        [sib, at_p(1), at_p(-1)]
        + [at_z(s)[1] for s in range(1, 8)]
        + [at_x(s)[1] for s in range(1, 4)]
        + [at_dp(s)[1] for s in range(1, 8)]
    )
    mine = pl.ds(pl.multiple_of(core * 128, 128), 128)
    sent = []

    value = cot_ref[...].astype(F32)
    for t, ref in ((1, wq_ref), (2, wk_ref), (3, wv_ref)):
        value = value + lax.dot_general(parts_ref[t, :, 0:AW], ref[...], NT, preferred_element_type=F32)
    here = xlo * 8 + z
    gh[here, mine, :] = value.astype(BF16)

    ways = {"up": (up_s, at_z(1)[1]), "down": (down_s, at_z(-1)[1]), "over": (over_s, over), "sib": (sib_s, sib)}
    count = {way: 0 for way in ways}

    def block(kind, dz):
        return (xlo if kind == "o" else 1 - xlo) * 8 + lax.rem(z + dz + 8, 8)

    def ship(u, *names):
        for way in names:
            sem, device = ways[way]
            ref = gh.at[u, mine, :]
            recv = sib_r if way == "sib" else own_r
            sent.append(send(ref, ref, sem.at[count[way]], recv.at[u], device))
            count[way] += 1

    def arrive(kind, dz, *names):
        u = block(kind, dz)
        ref = gh.at[u, mine, :]
        remote(ref, ref, up_s.at[0], own_r.at[u], sib).wait_recv()
        ship(u, *names)

    edge = gh.at[here]
    low = pl.ds(pl.multiple_of(core * 128, 64), 64)
    high = pl.ds(pl.multiple_of(core * 128 + 64, 64), 64)
    near = [
        send(edge.at[high, :], halo.at[0], halo_s.at[0], halo_r.at[0], at_p(1)),
        send(edge.at[low, :], halo.at[1], halo_s.at[1], halo_r.at[1], at_p(-1)),
    ]
    ship(here, "up", "down", "over", "sib")

    lane = lax.broadcasted_iota(jnp.int32, (128, 128), 1)
    left = lane < 64

    def chunk(t, n):
        return parts_ref[t, :, 128 * n : 128 * n + 128].astype(F32)

    def swap(a):
        return pltpu.roll(a, 64, axis=1)

    def put(ref, n, a):
        ref[:, 128 * n : 128 * n + 128] = a.astype(BF16)

    k0, k1, k2 = (swap(chunk(2, n)) for n in range(3))
    v0, v1, v2 = (swap(chunk(3, n)) for n in range(3))
    zero = jnp.zeros((128, 128), F32)
    for n, a in enumerate((chunk(1, 0), chunk(1, 1), jnp.where(left, chunk(1, 2), k0), jnp.where(left, k0, k1),
                           jnp.where(left, k1, k2))):
        put(dqk, n, a)
    for n, a in enumerate((chunk(3, 0), chunk(3, 1), chunk(3, 2), zero, zero)):
        put(dva, n, a)
    for n, a in enumerate((zero, zero, jnp.where(left, 0.0, v0), jnp.where(left, v0, v1), jnp.where(left, v1, v2))):
        put(dvb, n, a)
    turned[...] = hid_ref[...].astype(F32).T.astype(BF16)
    aturned[...] = parts_ref[0].astype(F32).T.astype(BF16)

    def keep(first_row, value):
        for n in range(5):
            start = 1280 * n + first_row
            xs[start : start + value.shape[0]] = value[:, 128 * n : 128 * n + 128].astype(BF16)

    def mm(a, b):
        return jnp.dot(a, b, preferred_element_type=F32)

    keep(0, mm(turned[0:320], dqk[...]))
    keep(320, mm(turned[320:640], dqk[...]))
    keep(640, mm(aturned[0:320], cot_ref[...]))
    keep(960, mm(turned[0:320], dva[...]) + mm(turned[320:640], dvb[...]))

    def part(c, k):
        return pl.ds(pl.multiple_of(c * 3200 + k * 800, 16), 800)

    pair = [send(xs.at[part(1 - core, k)], half.at[k], pair_s.at[k], pair_r.at[k], sib) for k in range(4)]
    arrive("o", -1, "up", "over", "sib")
    arrive("o", 1, "down", "over", "sib")
    arrive("p", 0, "sib")

    for copy in near:
        copy.wait()
    j = lax.broadcasted_iota(jnp.int32, (64, 640), 0)
    rows = (
        jnp.where(p > 0, halo[0].astype(F32), 0.0),
        gh[here, low, :].astype(F32),
        gh[here, high, :].astype(F32),
        jnp.where(p < 31, halo[1].astype(F32), 0.0),
    )
    for r in range(4):
        moved = shifted(rows[r], j)
        for b in range(3):
            sh[2 - b, 64 * r : 64 * r + 64] = moved[b].astype(BF16)

    def tap(t):
        a, b = t // 3, t % 3
        loads[t].wait()
        start = 64 * (2 - a)
        term = lax.dot_general(sh[b, start : start + 128], w[t], NT, preferred_element_type=F32)
        if t:
            acc[...] += term
        else:
            acc[...] = term

    for copy in pair:
        copy.wait()
    for k in range(4):
        half[k] = (half[k].astype(F32) + xs[part(core, k)].astype(F32)).astype(BF16)
    far = lax.rem(y + 2, 4)
    y_up, y_down = at_y(1), at_y(-1)
    sent.append(send(half.at[far, 0:400], ya, y_s.at[0], y_r.at[0], y_up[1]))
    sent.append(send(half.at[far, 400:800], yb, y_s.at[1], y_r.at[1], y_down[1]))
    tap(0)
    tap(1)
    arrive("o", -2, "up", "over", "sib")
    arrive("o", 2, "down", "over", "sib")
    remote(half.at[far, 0:400], ya, y_s.at[0], y_r.at[0], sib).wait_recv()
    remote(half.at[far, 400:800], yb, y_s.at[1], y_r.at[1], sib).wait_recv()
    half[y_up[0], 0:400] = (half[y_up[0], 0:400].astype(F32) + ya[...].astype(F32)).astype(BF16)
    half[y_down[0], 400:800] = (half[y_down[0], 400:800].astype(F32) + yb[...].astype(F32)).astype(BF16)
    sent.append(send(half.at[y_up[0]], yc, y_s.at[2], y_r.at[2], y_up[1]))
    sent.append(send(half.at[y_down[0]], yd, y_s.at[3], y_r.at[3], y_down[1]))
    tap(2)
    tap(3)
    arrive("p", -1, "sib")
    arrive("p", 1, "sib")
    tap(4)
    arrive("o", -3, "up", "sib")
    arrive("o", 3, "sib")
    remote(half.at[0], yc, y_s.at[2], y_r.at[2], sib).wait_recv()
    remote(half.at[0], yd, y_s.at[3], y_r.at[3], sib).wait_recv()
    plane[0:800] = (half[y].astype(F32) + yc[...].astype(F32) + yd[...].astype(F32)).astype(BF16)
    plane[800:1024] = jnp.zeros((224, 128), BF16)

    def quarter(k):
        return pl.ds(pl.multiple_of(k * 256, 256), 256)

    def slot(k):
        return pl.ds(pl.multiple_of(k * 32, 32), 32)

    crossing = []
    for s in range(1, 4):
        other, device = at_x(s)
        crossing.append(send(plane.at[quarter(other)], xin.at[s], x_s.at[s], x_r.at[s], device))
    tap(5)
    tap(6)
    arrive("p", -2, "up", "sib")
    arrive("p", 2, "down", "sib")
    whole = plane[quarter(x)].astype(F32)
    for s in range(1, 4):
        crossing[s - 1].wait()
        whole = whole + xin[s].astype(F32)
    xsum[...] = whole.astype(BF16)
    along = []
    for s in range(1, 8):
        other, device = at_z(s)
        along.append(send(xsum.at[slot(other)], zin.at[s], z_s.at[s], z_r.at[s], device))
    tap(7)
    tap(8)
    lat_ref[...] = acc[...].astype(BF16)
    arrive("o", 4, "sib")
    whole = xsum[slot(z)].astype(F32)
    for s in range(1, 8):
        along[s - 1].wait()
        whole = whole + zin[s].astype(F32)
    zfull[slot(z)] = whole.astype(BF16)
    zback = []
    for s in range(1, 8):
        ref = zfull.at[slot(z)]
        zback.append(send(ref, ref, zb_s.at[s], zb_r.at[s], at_z(s)[1]))

    def gain(kind, dz, start=False):
        u = block(kind, dz)
        ref = gh.at[u, pl.ds(pl.multiple_of((1 - core) * 128, 128), 128), :]
        remote(ref, ref, up_s.at[0], sib_r.at[u], sib).wait_recv()
        term = jnp.dot(lhs_ref[u], gh[u], preferred_element_type=F32)
        if start:
            prod[...] = term
        else:
            prod[...] += term

    gain("o", 0, True)
    gain("p", 0)
    arrive("p", -3, "sib")
    arrive("p", 3, "down", "sib")
    gain("o", -1)
    gain("o", 1)
    for copy in zback:
        copy.wait()
    pfull[quarter(x)] = zfull[...]
    xback = []
    for s in range(1, 4):
        ref = pfull.at[quarter(x)]
        xback.append(send(ref, ref, xb_s.at[s], xb_r.at[s], at_x(s)[1]))
    gain("p", -1)
    gain("p", 1)
    gain("o", -2)
    gain("o", 2)
    arrive("p", 4, "sib")
    for copy in xback:
        copy.wait()
    ob[part(core, y)] = pfull[0:800]

    def whole_part(k, send_sem, recv_sem, device):
        ref = ob.at[part(core, k)]
        return send(ref, ref, send_sem, recv_sem, device)

    def half_part(k, first, send_sem, recv_sem, device):
        start = core * 3200 + k * 800 + (0 if first else 400)
        ref = ob.at[pl.ds(pl.multiple_of(start, 16), 400)]
        return send(ref, ref, send_sem, recv_sem, device)

    sent.append(whole_part(y, yb_s.at[0], yb_r.at[0], y_up[1]))
    sent.append(whole_part(y, yb_s.at[1], yb_r.at[1], y_down[1]))
    fin = [whole_part(y, fin_s.at[0], fin_r.at[0], sib)]
    gain("o", -3)
    gain("o", 3)
    gain("p", -2)
    gain("p", 2)
    ref = ob.at[part(core, y_down[0])]
    remote(ref, ref, yb_s.at[0], yb_r.at[0], sib).wait_recv()
    ref = ob.at[part(core, y_up[0])]
    remote(ref, ref, yb_s.at[1], yb_r.at[1], sib).wait_recv()
    sent.append(half_part(y_down[0], True, yb_s.at[2], yb_r.at[2], y_up[1]))
    sent.append(half_part(y_up[0], False, yb_s.at[3], yb_r.at[3], y_down[1]))
    fin.append(whole_part(y_down[0], fin_s.at[1], fin_r.at[1], sib))
    fin.append(whole_part(y_up[0], fin_s.at[2], fin_r.at[2], sib))
    gain("o", 4)
    gain("p", -3)
    gain("p", 3)
    gain("p", 4)

    for t in range(9):
        small[20 * t : 20 * t + 20] = prod[32 * t : 32 * t + 20]
    small[180:192] = jnp.zeros((12, 640), F32)
    for n in range(5):
        piece = small[:, 128 * n : 128 * n + 128].astype(BF16)
        for i in range(12):
            f = 192 * n + 16 * i
            tb[f // 128, f % 128 : f % 128 + 16] = piece[16 * i : 16 * i + 16]
    tb[7, 64:128] = jnp.zeros((64, 128), BF16)
    there = []
    for s in range(1, 8):
        other, device = at_dp(s)
        there.append(send(tb.at[other], tin.at[s], t_s.at[s], t_r.at[s], device))
    ref = ob.at[pl.ds(pl.multiple_of(core * 3200 + far * 800, 16), 400)]
    remote(ref, ref, yb_s.at[2], yb_r.at[2], sib).wait_recv()
    ref = ob.at[pl.ds(pl.multiple_of(core * 3200 + far * 800 + 400, 16), 400)]
    remote(ref, ref, yb_s.at[3], yb_r.at[3], sib).wait_recv()
    fin.append(whole_part(far, fin_s.at[3], fin_r.at[3], sib))
    whole = tb[dp].astype(F32)
    for s in range(1, 8):
        there[s - 1].wait()
        whole = whole + tin[s].astype(F32)
    taps_ref[dp] = whole.astype(BF16)
    tback = []
    for s in range(1, 8):
        ref = taps_ref.at[dp]
        tback.append(send(ref, ref, u_s.at[s], u_r.at[s], at_dp(s)[1]))
    for copy in fin:
        copy.wait()
    for n in range(5):
        out_ref[:, 128 * n : 128 * n + 128] = ob[1280 * n : 1280 * n + 1280]
    for copy in sent:
        copy.wait_send()
    for copy in tback:
        copy.wait()


def finish(parts, hidden, cotangent, wq, wk, wv, lhs, taps):
    dma = pltpu.SemaphoreType.DMA
    vmem = pl.BlockSpec(memory_space=pltpu.VMEM)

    def b16(*shape):
        return pltpu.VMEM(shape, BF16)

    def f32(*shape):
        return pltpu.VMEM(shape, F32)

    return pl.pallas_call(
        finish_kernel,
        out_shape=(
            jax.ShapeDtypeStruct((1280, 640), BF16),
            jax.ShapeDtypeStruct((8, 128, 128), BF16),
            jax.ShapeDtypeStruct((128, 640), BF16),
        ),
        in_specs=[vmem] * 7 + [pl.BlockSpec(memory_space=pl.ANY)],
        out_specs=(vmem,) * 3,
        scratch_shapes=[
            b16(9, 640, 640), dma((9,)), b16(16, 256, 640), b16(2, 64, 640), b16(3, 256, 640), f32(128, 640),
            f32(288, 640), f32(192, 640), b16(128, 640), b16(128, 640), b16(128, 640), b16(640, 128), b16(384, 128),
            b16(6400, 128), b16(4, 800, 128), b16(400, 128), b16(400, 128), b16(800, 128), b16(800, 128),
            b16(1024, 128), b16(4, 256, 128), b16(256, 128), b16(8, 32, 128), b16(256, 128), b16(1024, 128),
            b16(6400, 128), b16(8, 128, 128), b16(8, 128, 128),
            dma((2,)), dma((2,)), dma((5,)), dma((5,)), dma((5,)), dma((16,)), dma((16,)), dma((16,)),
            dma((4,)), dma((4,)), dma((4,)), dma((4,)), dma((4,)), dma((4,)), dma((8,)), dma((8,)),
            dma((8,)), dma((8,)), dma((4,)), dma((4,)), dma((4,)), dma((4,)), dma((4,)), dma((4,)),
            dma((8,)), dma((8,)), dma((8,)), dma((8,)),
        ],
        compiler_params=pltpu.CompilerParams(
            collective_id=0, has_side_effects=True, vmem_limit_bytes=52 * 1024 * 1024
        ),
        name="finish",
    )(parts, hidden, cotangent, wq, wk, wv, lhs, taps)


def body(latent, cotangent, conv_weight, query_weight, key_weight, value_weight, out_weight):
    lat = latent.reshape(128, 640)
    cot = cotangent.reshape(128, 640)
    w = conv_weight.reshape(9, 640, 640)
    hidden, packed, lhs = first(lat, cot, query_weight, key_weight, value_weight, out_weight, w)
    parts = attend(packed)
    rows, taps, grad_latent = finish(parts, hidden, cot, query_weight, key_weight, value_weight, lhs, w)
    taps = taps.reshape(1024, 128)[:960].reshape(5, 192, 128)[:, :180].transpose(1, 0, 2)
    grad_conv = taps.reshape(3, 3, 20, 640).astype(F32)
    grad_value = jnp.concatenate([rows[960:, :320], rows[960:, 320:]], axis=0).astype(F32)
    return (
        grad_latent.reshape(latent.shape),
        grad_conv,
        rows[:640, :320].astype(F32),
        rows[:640, 320:].astype(F32),
        grad_value,
        rows[640:960].astype(F32),
    )


def solution(mesh):
    placed = (P("dp", "patch", None, None), P("dp", "patch", None, None), P(), P(), P(), P(), P())
    return jax.shard_map(
        body,
        mesh=mesh,
        in_specs=placed,
        out_specs=(P("dp", "patch", None, None), P(None, None, "patch", None), P(), P(), P(), P()),
        check_vma=False,
    )
```

time: 787 us -> 181 us (0.23)
  waiting for transfers between devices: 557 us -> 0 us
  Pallas kernels: 0 us -> 167 us
  matrix products: 99.4 us -> 0 us
  blocking collectives: 82.6 us -> 0 us
  between operations: 14.7 us -> 0.83 us
  starting transfers between devices: 9.46 us -> 0 us
    psum x2 -> x0, waiting for transfers between devices: 343 us -> none  [the longest x1 273 us: body(): lax.psum((outer_sum(hidden, grad_q), outer_sum(hidden, grad_k), outer_sum...]
    all_gather x5 -> x0, waiting for transfers between devices: 213 us -> none  [the longest x1 70.8 us: body(): lax.all_gather(key, 'patch', axis=0, tiled=True)]
    pallas_call x0 -> x3, Pallas kernels: none -> 167 us  [the longest x1 72.2 us: finish(): pl.pallas_call(finish_kernel, out_shape=(jax.ShapeDtypeStruct((1280, 640)...]
    dot_general x44 -> x0, matrix products: 99.4 us -> none  [the longest x13 21.3 us: outer_sum(): lax.dot_general(left, right, (((0,), (0,)), ((), ())), preferred_element_...]
    all_gather x2 -> x0, blocking collectives: 66.7 us -> none  [the longest x1 35.5 us: body(): lax.all_gather(delta.T, 'patch', axis=0, tiled=True)]
    all_to_all x1 -> x0, blocking collectives: 15.9 us -> none  [body(): lax.all_to_all(latent[0], 'patch', split_axis=2, concat_axis=0, tiled=True)]
    ppermute x4 -> x0, starting transfers between devices: 9.18 us -> none  [the longest x2 6.33 us: with_halo(): before = lax.ppermute(last, axis, up)]
  transfers between devices with their start and end apart: 11 -> 0, of which waited for: 7 -> 0; matrix products, arithmetic and copies ran while one was open for 9% -> 0% of each run, Pallas kernels for 0% -> 0%
where the time goes in v1:
time: 181 us; the launch traced here: 180 us
  Pallas kernels  167 us (92%)
  local copies, waits for them, and re-layouts  10.3 us (6%)
  other arithmetic  2.48 us (1%)
    pallas_call x1, Pallas kernels, finish(): pl.pallas_call(finish_kernel, out_shape=(jax.ShapeDtypeStruct((1280, 640)...  72.2 us
    pallas_call x1, Pallas kernels, attend(): pl.pallas_call(attend_kernel, out_shape=jax.ShapeDtypeStruct((4, 128, 384...  71.9 us
    pallas_call x1, Pallas kernels, first(): pl.pallas_call(first_kernel, out_shape=(jax.ShapeDtypeStruct((128, 640),...  22.6 us
    unnamed x23, local copies, waits for them, and re-layouts  9.1 us

profile of v1, /device:TPU:8, one launch (start us, length us, event | category | flops | bytes accessed | tf_op | source)
XLA Modules:
  0.0 180.3 jit_solution(12469856907354289415)
XLA Ops:
  0.6 0.0 copy-start.4
  0.6 0.0 copy-start.7
  0.7 0.0 copy-start.3
  0.7 0.0 copy-start.5
  0.7 1.3 copy.32.wq_ref
  2.0 1.3 copy.33.wk_ref
  3.3 0.0 copy-done.7
  3.3 0.0 copy-start
  3.3 0.3 copy.34.wv_ref
  3.6 0.0 copy-done.4
  3.6 0.0 copy-done.3
  3.6 0.0 copy-done.5
  3.6 0.0 copy-start.1
  3.6 22.6 %first.1 = (bf16[128,640]{1,0:T(8,128)(2,1)S(1)}, bf16[4,4,128,128]{3,2,1,0:T(8,128)(2,1)S(1)}, bf16[16,288,256]{2,1,0:T(8,128)(2,1)S(1)}) custom-call(bf16[128,640]{1,0:T(8,128)(2,1)S(1)} %bitcast.12, bf16[128,640]{1,0:T(8,128)(2,1)S(1)} %bitcast.8, bf16[640,320]{1,0:T(8,128)(2,1)S(1)} %copy.32.wq_ref, bf16[640,320]{1,0:T(8,128)(2,1)S(1)} %copy.33.wk_ref, ...), custom_call_target="tpu_custom_call" | custom-call | tf_op jit(solution)/shard_map/first/pallas_call | solution.py:401
  26.2 0.0 copy-done
  26.3 0.0 copy-done.1
  26.3 0.0 copy-start.2
  26.3 1.4 copy-done.2
  27.7 71.9 %attend.1.parts_ref = bf16[4,128,384]{2,1,0:T(8,128)(2,1)S(1)} custom-call(bf16[4,4,128,128]{3,2,1,0:T(8,128)(2,1)S(1)} %get-tuple-element.12.x_ref), custom_call_target="tpu_custom_call" | custom-call | tf_op jit(solution)/shard_map/attend/pallas_call | solution.py:238
  99.6 72.2 %finish.1 = (bf16[1280,640]{1,0:T(8,128)(2,1)}, bf16[8,128,128]{2,1,0:T(8,128)(2,1)S(1)}, bf16[128,640]{1,0:T(8,128)(2,1)S(1)}) custom-call(bf16[4,128,384]{2,1,0:T(8,128)(2,1)S(1)} %attend.1.parts_ref, bf16[128,640]{1,0:T(8,128)(2,1)S(1)} %get-tuple-element.13.hid_ref, bf16[128,640]{1,0:T(8,128)(2,1)S(1)} %bitcast.9, bf16[640,320]{1,0:T(8,128)(2,1)S(1)} %copy.32.wq_ref, ...), custom_call_target="tpu_custom_call" | custom-call | tf_op jit(solution)/shard_map/finish/pallas_call | solution.py:754
  171.8 0.0 copy-start.6
  171.8 0.1 copy.38
  172.0 0.9 reshape.39
  172.9 0.5 copy-done.6
  173.4 0.1 fusion
  173.6 0.1 maximum_convert_fusion
  173.6 1.2 copy.41
  174.8 0.9 slice_convert_fusion.2
  175.8 1.4 slice_convert_fusion
  177.2 1.2 copy.40
  178.4 1.2 copy.39
  179.6 0.7 copy.43
  (2 shorter events, 0.1 us)
Async XLA Ops:
  0.6 3.0 %copy-start.4 = (bf16[320,640]{1,0:T(8,128)(2,1)S(1)}, bf16[320,640]{1,0:T(8,128)(2,1)}, u32[]{:S(2)}) copy-start(bf16[320,640]{1,0:T(8,128)(2,1)} %wo_ref.1) | copy-start | bytes 1228804
  0.6 2.7 %copy-start.7 = (bf16[640,320]{0,1:T(8,128)(2,1)S(1)}, bf16[640,320]{0,1:T(8,128)(2,1)}, u32[]{:S(2)}) copy-start(bf16[640,320]{0,1:T(8,128)(2,1)} %param.12) | copy-start | bytes 1228804
  0.7 2.9 %copy-start.3 = (bf16[1,2,64,640]{3,2,1,0:T(8,128)(2,1)S(1)}, bf16[1,2,64,640]{3,2,1,0:T(8,128)(2,1)}, u32[]{:S(2)}) copy-start(bf16[1,2,64,640]{3,2,1,0:T(8,128)(2,1)} %param.8) | copy-start | bytes 491524
  0.7 2.9 %copy-start.5 = (bf16[1,2,64,640]{3,2,1,0:T(8,128)(2,1)S(1)}, bf16[1,2,64,640]{3,2,1,0:T(8,128)(2,1)}, u32[]{:S(2)}) copy-start(bf16[1,2,64,640]{3,2,1,0:T(8,128)(2,1)} %param.7) | copy-start | bytes 491524
  3.3 22.9 %copy-start = (bf16[640,320]{1,0:T(8,128)(2,1)}, bf16[640,320]{1,0:T(8,128)(2,1)S(1)}, u32[]{:S(2)}) copy-start(bf16[640,320]{1,0:T(8,128)(2,1)S(1)} %copy.33.wk_ref) | copy-start | bytes 1228804
  3.6 22.6 %copy-start.1 = (bf16[640,320]{1,0:T(8,128)(2,1)}, bf16[640,320]{1,0:T(8,128)(2,1)S(1)}, u32[]{:S(2)}) copy-start(bf16[640,320]{1,0:T(8,128)(2,1)S(1)} %copy.34.wv_ref) | copy-start | bytes 1228804
  26.3 1.4 copy-start.2
  171.8 1.6 copy-start.6

commit v2 on v1

v2 whole, which is shorter than its diff:
```python
import functools
import jax
import jax.numpy as jnp
from jax import lax
from jax.experimental import pallas as pl
from jax.experimental.pallas import tpu as pltpu
from jax.sharding import PartitionSpec as P

NH = 5
HD = 64
AW = 320
MESH = pl.DeviceIdType.MESH
F32 = jnp.float32
BF16 = jnp.bfloat16


def place():
    p = lax.axis_index("patch")
    return lax.axis_index("dp"), p // 16, lax.rem(p, 16) // 2, lax.rem(p, 2)


def send(src, dst, send_sem, recv_sem, device):
    copy = pltpu.make_async_remote_copy(
        src_ref=src, dst_ref=dst, send_sem=send_sem, recv_sem=recv_sem,
        device_id=device, device_id_type=MESH,
    )
    copy.start()
    return copy


NT = (((1,), (1,)), ((), ()))
LOG2E = 1.4426950408889634


def remote(src, dst, send_sem, recv_sem, device):
    return pltpu.make_async_remote_copy(
        src_ref=src, dst_ref=dst, send_sem=send_sem, recv_sem=recv_sem,
        device_id=device, device_id_type=MESH,
    )


def attend_kernel(windows, lhs_ref, x_ref, out_ref, kv, kvt, qd, qs, gs, q4, g4, gt, gt4, scores, slope, pb, sb,
                  top, low, att, delta, dq, top4, low4, att4, delta4, dq4, part, box_up, box_down, ahead, behind,
                  mix, mix_in, stat, own4, stage, res,
                  kv_s, kv_r, qd_s, qd_r, up_s, up_r, down_s, down_r, rup_s, rup_r, rdown_s, rdown_r,
                  mix_s, mix_r, stat_s, stat_r, g_s, g_r):
    dp, xlo, z, core = place()
    j = xlo * 2 + core

    def at_z(step):
        return (dp, xlo * 16 + lax.rem(z + step + 8, 8) * 2 + core)

    def in_quad(step):
        m = lax.rem(j + step, 4)
        return m, (dp, (m // 2) * 16 + z * 2 + lax.rem(m, 2))

    def rows(m):
        return pl.ds(pl.multiple_of(m * 128, 128), 128)

    first, second = [], []
    for s in range(1, 4):
        m, device = in_quad(s)
        first.append(send(x_ref.at[2 * m], kv.at[z, rows(j), :], kv_s.at[s], kv_r.at[s], device))
    for s in range(1, 4):
        m, device = in_quad(s)
        second.append(send(x_ref.at[2 * m + 1], qd.at[0, rows(j), :], qd_s.at[0, s], qd_r.at[0, s], device))
        second.append(send(x_ref.at[8], qd.at[1, rows(j), :], qd_s.at[1, s], qd_r.at[1, s], device))
    kv[z, rows(j), :] = x_ref[2 * j]
    kv[z, 512:640] = x_ref[9]
    qd[0, rows(j), :] = x_ref[2 * j + 1]
    qd[1, rows(j), :] = x_ref[8]
    lane = lax.broadcasted_iota(jnp.int32, (128, 128), 1)
    left = lane < 64
    for ref in (top, top4):
        ref[...] = jnp.full(ref.shape, -jnp.inf, F32)
    for ref in (low, low4, att, att4, dq, dq4):
        ref[...] = jnp.zeros(ref.shape, F32)

    def ring_up(s):
        k = lax.rem(z + 8 - s, 8)
        ref = kv.at[k] if s < 3 else kv.at[k, 0:320]
        return remote(ref, ref, up_s.at[s], up_r.at[s], at_z(1))

    def ring_down(s):
        k = lax.rem(z + s, 8)
        ref = kv.at[k] if s < 3 else kv.at[k, 320:640]
        return remote(ref, ref, down_s.at[s], down_r.at[s], at_z(-1))

    for copy in first:
        copy.wait()
    ring_up(0).start()
    ring_down(0).start()
    windows(lhs_ref)
    for copy in second:
        copy.wait()
    for m in range(4):
        r = slice(m * 128, m * 128 + 128)
        for i, (a, b, bt) in enumerate(((qs, gs, gt), (q4, g4, gt4))):
            pair = qd[i, r].astype(F32)
            a[r] = jnp.where(left, pair, 0.0).astype(BF16)
            b[r] = jnp.where(left, 0.0, pair).astype(BF16)
            bt[:, r] = pair.T[64:128]

    def soften(b, keys, q, top, low, att):
        s = scores[b, keys, q]
        old = top[:, q]
        new = jnp.maximum(old, jnp.max(s, axis=0, keepdims=True))
        p = jnp.exp2(s - new)
        fade = jnp.exp2(old - new)
        low[:, q] = low[:, q] * fade + jnp.sum(p, axis=0, keepdims=True)
        top[:, q] = new
        att[:, q] = att[:, q] * fade
        pb[keys, q] = p.astype(BF16)

    main, side = slice(0, 512), slice(512, 640)
    quarters = [slice(128 * i, 128 * i + 128) for i in range(4)]

    def pass_one(t, carry):
        for s in range(3):
            @pl.when(t == 2 * s + 1)
            def _():
                ring_up(s).wait_recv()
                ring_up(s + 1).start()

            @pl.when(t == 2 * s + 2)
            def _():
                ring_down(s).wait_recv()
                ring_down(s + 1).start()

        @pl.when(t == 7)
        def _():
            ring_up(3).wait_recv()
            ring_down(3).wait_recv()

        offset = jnp.where(lax.rem(t, 2) == 1, 8 - (t + 1) // 2, t // 2)
        b = lax.rem(z + offset, 8)
        scores[b, main] = lax.dot_general(kv[b, main], qs[...], NT, preferred_element_type=F32) * LOG2E
        scores[b, side] = lax.dot_general(kv[b, side], q4[...], NT, preferred_element_type=F32) * LOG2E
        for i in range(5):
            c = slice(128 * i, 128 * i + 128)
            kvt[b, :, c] = kv[b, c].astype(F32).T.astype(BF16)
        for q in quarters:
            soften(b, main, q, top, low, att)
            soften(b, side, q, top4, low4, att4)
        att[...] += jnp.dot(kvt[b, 64:128, main], pb[main], preferred_element_type=F32)
        att4[...] += jnp.dot(kvt[b, 64:128, side], pb[side], preferred_element_type=F32)
        return carry

    lax.fori_loop(0, 8, pass_one, 0)
    for m in range(4):
        q = quarters[m]
        mix[m, 0:64] = att4[:, q]
        mix[m, 64:65] = top4[:, q]
        mix[m, 65:66] = low4[:, q]
        mix[m, 66:72] = jnp.zeros((6, 128), F32)
    mixing = []
    for s in range(1, 4):
        m, device = in_quad(s)
        mixing.append(send(mix.at[m], mix_in.at[s], mix_s.at[s], mix_r.at[s], device))
    mix_in[0] = mix[j]
    att[...] = att[...] / low[...]
    top[...] = top[...] + jnp.log2(low[...])
    delta[...] = jnp.sum(att[...] * gt[...], axis=0, keepdims=True)

    def stat_copy(s):
        return remote(stat.at[j], stat.at[j], stat_s.at[s], stat_r.at[s], in_quad(s)[1])

    for copy in mixing:
        copy.wait()
    tops = [mix_in[s, 64:65] for s in range(4)]
    best = jnp.maximum(jnp.maximum(tops[0], tops[1]), jnp.maximum(tops[2], tops[3]))
    total, blend = jnp.zeros((1, 128), F32), jnp.zeros((64, 128), F32)
    for s in range(4):
        weight = jnp.exp2(tops[s] - best)
        total = total + mix_in[s, 65:66] * weight
        blend = blend + mix_in[s, 0:64] * weight
    blend = blend / total
    own4[0:64] = blend
    own4[64:128] = jnp.zeros((64, 128), F32)
    stat[j, 0:1] = best + jnp.log2(total)
    stat[j, 1:2] = jnp.sum(blend * gt4[:, rows(j)], axis=0, keepdims=True)
    stat[j, 2:8] = jnp.zeros((6, 128), F32)
    for s in range(1, 4):
        stat_copy(s).start()

    def sum_up(s):
        r = slice(0, 320) if s == 0 else slice(0, 640)
        return remote(box_up.at[s, r], ahead.at[s, r], rup_s.at[s], rup_r.at[s], at_z(1))

    def sum_down(s):
        r = slice(320, 640) if s == 0 else slice(0, 640)
        return remote(box_down.at[s, r], behind.at[s, r], rdown_s.at[s], rdown_r.at[s], at_z(-1))

    def slopes(b, keys, q, top, delta):
        p = jnp.exp2(scores[b, keys, q] - top[:, q])
        pb[keys, q] = p.astype(BF16)
        sb[keys, q] = (p * (slope[keys, q] - delta[:, q])).astype(BF16)

    def pass_two(t, carry):
        offset = jnp.where(lax.rem(t, 2) == 0, 4 + t // 2, 4 - (t + 1) // 2)
        b = lax.rem(z + offset, 8)
        slope[main] = lax.dot_general(kv[b, main], gs[...], NT, preferred_element_type=F32)
        slope[side] = lax.dot_general(kv[b, side], g4[...], NT, preferred_element_type=F32)
        for q in quarters:
            slopes(b, main, q, top, delta)
        dq[...] += jnp.dot(kvt[b, 0:64, main], sb[main], preferred_element_type=F32)
        part[main] = jnp.dot(sb[main], qs[...], preferred_element_type=F32) + jnp.dot(
            pb[main], gs[...], preferred_element_type=F32
        )

        @pl.when(t == 0)
        def _():
            for s in range(1, 4):
                stat_copy(s).wait()
            for m in range(4):
                top4[:, quarters[m]] = stat[m, 0:1]
                delta4[:, quarters[m]] = stat[m, 1:2]

        for q in quarters:
            slopes(b, side, q, top4, delta4)
        dq4[...] += jnp.dot(kvt[b, 0:64, side], sb[side], preferred_element_type=F32)
        part[side] = jnp.dot(sb[side], q4[...], preferred_element_type=F32) + jnp.dot(
            pb[side], g4[...], preferred_element_type=F32
        )

        @pl.when(t == 0)
        def _():
            box_up[0, 0:320] = part[0:320].astype(BF16)
            sum_up(0).start()
            box_down[0, 320:640] = part[320:640].astype(BF16)
            sum_down(0).start()

        @pl.when(t == 1)
        def _():
            sum_up(0).wait_recv()
            box_up[1, 0:320] = (part[0:320] + ahead[0, 0:320].astype(F32)).astype(BF16)
            box_up[1, 320:640] = part[320:640].astype(BF16)
            sum_up(1).start()

        @pl.when(t == 2)
        def _():
            sum_down(0).wait_recv()
            box_down[1, 0:320] = part[0:320].astype(BF16)
            box_down[1, 320:640] = (part[320:640] + behind[0, 320:640].astype(F32)).astype(BF16)
            sum_down(1).start()

        for s in range(1, 3):
            @pl.when(t == 2 * s + 1)
            def _():
                sum_up(s).wait_recv()
                box_up[s + 1] = (part[...] + ahead[s].astype(F32)).astype(BF16)
                sum_up(s + 1).start()

            @pl.when(t == 2 * s + 2)
            def _():
                sum_down(s).wait_recv()
                box_down[s + 1] = (part[...] + behind[s].astype(F32)).astype(BF16)
                sum_down(s + 1).start()

        return carry

    lax.fori_loop(0, 8, pass_two, 0)
    for q in quarters:
        both = jnp.concatenate([dq[:, q] * HD ** -0.5, att[:, q]], axis=0)
        stage[0, q] = both.T.astype(BF16)
        both = jnp.concatenate([dq4[:, q] * HD ** -0.5, jnp.zeros((64, 128), F32)], axis=0)
        stage[1, q] = both.T.astype(BF16)
    late = []
    for s in range(1, 4):
        m, device = in_quad(s)
        late.append(send(stage.at[0:2, rows(m), :], res.at[j, 0:2], g_s.at[0, s], g_r.at[0, s], device))
    sum_up(3).wait_recv()
    sum_down(3).wait_recv()
    stage[2] = (part[main] + ahead[3, main].astype(F32) + behind[3, main].astype(F32)).astype(BF16)
    for s in range(1, 4):
        m, device = in_quad(s)
        late.append(send(stage.at[2, rows(m), :], res.at[j, 2], g_s.at[1, s], g_r.at[1, s], device))
    own = part[side] + ahead[3, side].astype(F32) + behind[3, side].astype(F32)
    for t in range(3):
        res[j, t] = stage[t, rows(j), :]
    for s in range(4):
        ring_up(s).wait_send()
        ring_down(s).wait_send()
        sum_up(s).wait_send()
        sum_down(s).wait_send()
    for copy in late:
        copy.wait()

    def swap(a):
        return pltpu.roll(a, 64, axis=1)

    for t, source, high in ((0, 0, True), (1, 0, False), (2, 2, False), (3, 2, True)):
        for i in range(2):
            a, b = res[2 * i, source].astype(F32), res[2 * i + 1, source].astype(F32)
            pair = jnp.where(left, swap(a), b) if high else jnp.where(left, a, swap(b))
            out_ref[t, :, 128 * i : 128 * i + 128] = pair.astype(BF16)
    last4 = (
        own4[...].T,
        sum(res[m, 1].astype(F32) for m in range(4)),
        own,
        swap(own),
    )
    for t in range(4):
        out_ref[t, :, 256:384] = jnp.where(left, last4[t], 0.0).astype(BF16)


def shifted(rows, j):
    before = jnp.where(j == 0, 0.0, pltpu.roll(rows, 1, axis=0))
    after = jnp.where(j == 63, 0.0, pltpu.roll(rows, 63, axis=0))
    return before, rows, after


def first_kernel(hbm, lat_ref, cot_ref, wq_ref, wk_ref, wv_ref, wo_ref, w, hid_ref, x_ref, load_sem, w_sem,
                 halo, turned, sbuf, share, sh, acc, tmp, halo_s, halo_r, share_s, share_r, rim_s, rim_r):
    dp, xlo, z, core = place()
    p = lax.axis_index("patch")
    spot = dp * 2 + xlo
    index = lax.rem(p, 16)

    def at(step):
        other = lax.rem(p + step + 32, 32)
        return (dp, other)

    local = (lat_ref, cot_ref, wo_ref, wk_ref, wv_ref, wq_ref)
    inputs = []
    for i, ref in enumerate(local):
        copy = pltpu.make_async_copy(hbm[i], ref, load_sem.at[i])
        copy.start()
        inputs.append(copy)
    loads = []
    for t in range(9):
        copy = pltpu.make_async_copy(hbm[6].at[t], w.at[t], w_sem.at[t])
        copy.start()
        loads.append(copy)
    barrier = pltpu.get_barrier_semaphore()

    def hello(s, carry):
        pl.semaphore_signal(barrier, inc=1, device_id=at(s), device_id_type=MESH)
        return carry

    def hello_plane(s, carry):
        other = lax.rem(spot + s, 16)
        device = (other // 2, lax.rem(other, 2) * 16 + index)
        pl.semaphore_signal(barrier, inc=1, device_id=device, device_id_type=MESH)
        return carry

    lax.fori_loop(1, 32, hello, 0)
    lax.fori_loop(1, 16, hello_plane, 0)
    inputs[0].wait()
    turned[0:640] = lat_ref[...].astype(F32).T
    turned[640:656] = jnp.zeros((16, 128), F32)
    for k in range(32):
        sbuf[k % 16, k // 16] = turned[20 * k : 20 * k + 32].astype(BF16)
    share[jnp.where(xlo == 0, 0, 17)] = jnp.zeros((2, 32, 128), BF16)
    share[index + 1] = sbuf[index]
    pl.semaphore_wait(barrier, 46)
    near = [
        send(lat_ref.at[64:128], halo.at[0], halo_s.at[0], halo_r.at[0], at(1)),
        send(lat_ref.at[0:64], halo.at[1], halo_s.at[1], halo_r.at[1], at(-1)),
    ]

    def share_copy(s):
        other = lax.rem(index + s, 16)
        return remote(sbuf.at[other], share.at[index + 1], share_s.at[s], share_r.at[s], (dp, xlo * 16 + other))

    rim = index == jnp.where(xlo == 0, 15, 0)
    rim_slot = jnp.where(xlo == 0, 0, 17)

    def rim_copy(s):
        return remote(sbuf.at[s], share.at[rim_slot], rim_s.at[s], rim_r.at[0], (dp, (1 - xlo) * 16 + s))

    def share_start(s, carry):
        share_copy(s).start()
        return carry

    def rim_start(s, carry):
        rim_copy(s).start()
        return carry

    lax.fori_loop(1, 16, share_start, 0)

    @pl.when(rim)
    def _():
        lax.fori_loop(0, 16, rim_start, 0)

    lane = lax.broadcasted_iota(jnp.int32, (128, 128), 1)
    left = lane < 64

    def pack(low_value, high_value, first_slot, last_slot):
        for n in range(3):
            c = slice(128 * n, min(128 * n + 128, AW))
            width = c.stop - c.start
            tmp[0, :, 0:width] = low_value[:, c]
            tmp[1, :, 0:width] = high_value[:, c]
            a, b = tmp[0], tmp[1]
            even = jnp.where(left, a, pltpu.roll(b, 64, axis=1)).astype(BF16)
            if n == 2:
                x_ref[last_slot] = even
            else:
                x_ref[4 * n + first_slot] = even
                x_ref[4 * n + 2 + first_slot] = jnp.where(left, pltpu.roll(a, 64, axis=1), b).astype(BF16)

    inputs[1].wait()
    inputs[2].wait()
    out_grad = lax.dot_general(cot_ref[...], wo_ref[...], NT, preferred_element_type=F32)
    tmp[...] = jnp.zeros(tmp.shape, F32)
    for copy in near:
        copy.wait()
    j = lax.broadcasted_iota(jnp.int32, (64, 640), 0)
    rows = (
        jnp.where(p > 0, halo[0].astype(F32), 0.0),
        lat_ref[0:64].astype(F32),
        lat_ref[64:128].astype(F32),
        jnp.where(p < 31, halo[1].astype(F32), 0.0),
    )
    for r in range(4):
        moved = shifted(rows[r], j)
        for b in range(3):
            sh[b, 64 * r : 64 * r + 64] = moved[b].astype(BF16)
    for t in range(9):
        a, b = t // 3, t % 3
        loads[t].wait()
        term = jnp.dot(sh[b, 64 * a : 64 * a + 128], w[t], preferred_element_type=F32)
        if t:
            acc[...] += term
        else:
            acc[...] = term
    hid_ref[...] = acc[...].astype(BF16)
    for copy in inputs[3:]:
        copy.wait()

    def project(ref):
        value = lax.dot_general(hid_ref[...], ref[...], NT, preferred_element_type=F32)
        return value.astype(BF16).astype(F32)

    pack(project(wk_ref), project(wv_ref), 0, 9)
    pack(project(wq_ref) * HD ** -0.5, out_grad, 1, 8)

    def windows(lhs_ref):
        def share_end(s, carry):
            share_copy(s).wait()
            return carry

        def rim_end(s, carry):
            rim_copy(s).wait_send()
            return carry

        lax.fori_loop(1, 16, share_end, 0)
        rim_copy(0).wait_recv()

        @pl.when(rim)
        def _():
            lax.fori_loop(0, 16, rim_end, 0)

        col = lax.broadcasted_iota(jnp.int32, (32, 128), 1)
        near_side = col < 64
        col = lax.rem(col, 64)

        def one(q, carry):
            lanes = pl.ds(pl.multiple_of(lax.rem(q, 2) * 128, 128), 128)
            for c in range(2):
                here = share[q + 1, c].astype(F32)
                turn = pltpu.roll(here, 64, axis=1)
                above = jnp.where(near_side, pltpu.roll(share[q, c].astype(F32), 64, axis=1), turn)
                below = jnp.where(near_side, turn, pltpu.roll(share[q + 2, c].astype(F32), 64, axis=1))
                for a, value in enumerate((above, here, below)):
                    three = (
                        jnp.where(col == 0, 0.0, pltpu.roll(value, 1, axis=1)),
                        value,
                        jnp.where(col == 63, 0.0, pltpu.roll(value, 127, axis=1)),
                    )
                    for b in range(3):
                        row = 288 * c + 32 * (3 * a + b)
                        lhs_ref[q // 2, row : row + 32, lanes] = three[b].astype(BF16)
            return carry

        lax.fori_loop(0, 16, one, 0)

    return windows


def finish_kernel(parts_ref, hid_ref, cot_ref, wq_ref, wk_ref, wv_ref, lhs_ref, w, out_ref, taps_ref, lat_ref,
                  gh, halo, sh, acc, prod, small, turned, xs, half, ya, yb, yc, yd,
                  plane, xin, xsum, zin, zfull, pfull, tb, tin, tfull, halo_s, halo_r, up_s, down_s, sib_s, own_r, sib_r,
                  pair_s, pair_r, y_s, y_r, x_s, x_r, z_s, z_r, zb_s, zb_r, xb_s, xb_r, yb_s, yb_r, fin_s, fin_r,
                  t_s, t_r, u_s, u_r):
    dp, xlo, z, core = place()
    p = lax.axis_index("patch")
    xhi, y = dp // 4, lax.rem(dp, 4)
    x = xhi * 2 + xlo
    sib = (dp, xlo * 16 + z * 2 + 1 - core)

    def at_z(s):
        other = lax.rem(z + s + 8, 8)
        return other, (dp, xlo * 16 + other * 2 + core)

    def at_y(s):
        other = lax.rem(y + s + 4, 4)
        return other, (xhi * 4 + other, p)

    def at_x(s):
        other = lax.rem(x + s, 4)
        return other, (other // 2 * 4 + y, lax.rem(other, 2) * 16 + z * 2 + core)

    spot = dp * 2 + xlo

    def at_spot(s):
        other = lax.rem(spot + s, 16)
        return other, (other // 2, lax.rem(other, 2) * 16 + z * 2 + core)

    def at_dp(s):
        other = lax.rem(dp + s, 8)
        return other, (other, p)

    def at_p(s):
        return (dp, lax.rem(p + s + 32, 32))

    mine = pl.ds(pl.multiple_of(core * 128, 128), 128)
    sent = []

    value = cot_ref[...].astype(F32)
    for t, ref in ((1, wq_ref), (2, wk_ref), (3, wv_ref)):
        value = value + jnp.dot(parts_ref[t, :, 0:AW], ref[...], preferred_element_type=F32)
    gh[z, mine, :] = value.astype(BF16)

    ways = {"up": (up_s, at_z(1)[1]), "down": (down_s, at_z(-1)[1]), "sib": (sib_s, sib)}
    count = {way: 0 for way in ways}
    low = pl.ds(pl.multiple_of(core * 128, 64), 64)
    high = pl.ds(pl.multiple_of(core * 128 + 64, 64), 64)

    def block(dz):
        return lax.rem(z + dz + 8, 8)

    def ship(dz, *names):
        u = block(dz)
        for way in names:
            sem, device = ways[way]
            ref = gh.at[u, mine, :]
            recv = (sib_r if way == "sib" else own_r).at[u]
            if dz == -3 and way == "up":
                ref, recv = gh.at[u, low, :], own_r.at[8]
            if dz == 3 and way == "down":
                ref, recv = gh.at[u, high, :], own_r.at[9]
            sent.append(send(ref, ref, sem.at[count[way]], recv, device))
            count[way] += 1

    def arrive(dz, *names):
        u = block(dz)
        if dz == 4:
            ref = gh.at[u, low, :]
            remote(ref, ref, up_s.at[0], own_r.at[8], sib).wait_recv()
            ref = gh.at[u, high, :]
            remote(ref, ref, up_s.at[0], own_r.at[9], sib).wait_recv()
        else:
            ref = gh.at[u, mine, :]
            remote(ref, ref, up_s.at[0], own_r.at[u], sib).wait_recv()
        ship(dz, *names)

    edge = gh.at[z]
    near = [
        send(edge.at[high, :], halo.at[0], halo_s.at[0], halo_r.at[0], at_p(1)),
        send(edge.at[low, :], halo.at[1], halo_s.at[1], halo_r.at[1], at_p(-1)),
    ]
    ship(0, "up", "down", "sib")

    for i, t in enumerate((1, 2, 3, 0)):
        turned[...] = parts_ref[t].astype(F32).T.astype(BF16)
        right = hid_ref if t else cot_ref
        xs[AW * i : AW * i + AW] = jnp.dot(turned[0:AW], right[...], preferred_element_type=F32).astype(BF16)

    def part(c, k):
        return pl.ds(pl.multiple_of(c * 640 + k * 160, 16), 160)

    pair = [send(xs.at[part(1 - core, k)], half.at[k], pair_s.at[k], pair_r.at[k], sib) for k in range(4)]
    arrive(-1, "up", "sib")
    arrive(1, "down", "sib")

    for copy in near:
        copy.wait()
    j = lax.broadcasted_iota(jnp.int32, (64, 640), 0)
    rows = (
        jnp.where(p > 0, halo[0].astype(F32), 0.0),
        gh[z, low, :].astype(F32),
        gh[z, high, :].astype(F32),
        jnp.where(p < 31, halo[1].astype(F32), 0.0),
    )
    for r in range(4):
        moved = shifted(rows[r], j)
        for b in range(3):
            sh[2 - b, 64 * r : 64 * r + 64] = moved[b].astype(BF16)

    def tap(t):
        a, b = t // 3, t % 3
        start = 64 * (2 - a)
        term = lax.dot_general(sh[b, start : start + 128], w[t], NT, preferred_element_type=F32)
        if t:
            acc[...] += term
        else:
            acc[...] = term

    def gain(dz, start=False):
        u = block(dz)
        ref = gh.at[u, pl.ds(pl.multiple_of((1 - core) * 128, 128), 128), :]
        remote(ref, ref, up_s.at[0], sib_r.at[u], sib).wait_recv()
        term = jnp.dot(lhs_ref[u], gh[u], preferred_element_type=F32)
        if start:
            prod[...] = term
        else:
            prod[...] += term

    tap(0)
    for copy in pair:
        copy.wait()
    for k in range(4):
        half[k] = (half[k].astype(F32) + xs[part(core, k)].astype(F32)).astype(BF16)
    far = lax.rem(y + 2, 4)
    y_up, y_down = at_y(1), at_y(-1)
    sent.append(send(half.at[far, 0:80], ya, y_s.at[0], y_r.at[0], y_up[1]))
    sent.append(send(half.at[far, 80:160], yb, y_s.at[1], y_r.at[1], y_down[1]))
    tap(1)
    arrive(-2, "up", "sib")
    arrive(2, "down", "sib")
    remote(half.at[far, 0:80], ya, y_s.at[0], y_r.at[0], sib).wait_recv()
    remote(half.at[far, 80:160], yb, y_s.at[1], y_r.at[1], sib).wait_recv()
    half[y_up[0], 0:80] = (half[y_up[0], 0:80].astype(F32) + ya[...].astype(F32)).astype(BF16)
    half[y_down[0], 80:160] = (half[y_down[0], 80:160].astype(F32) + yb[...].astype(F32)).astype(BF16)
    sent.append(send(half.at[y_up[0]], yc, y_s.at[2], y_r.at[2], y_up[1]))
    sent.append(send(half.at[y_down[0]], yd, y_s.at[3], y_r.at[3], y_down[1]))
    tap(2)
    gain(0, True)
    arrive(-3, "up", "sib")
    arrive(3, "down", "sib")
    gain(-1)
    remote(half.at[0], yc, y_s.at[2], y_r.at[2], sib).wait_recv()
    remote(half.at[0], yd, y_s.at[3], y_r.at[3], sib).wait_recv()
    for n in range(5):
        c = slice(128 * n, 128 * n + 128)
        whole = half[y, :, c].astype(F32) + yc[:, c].astype(F32) + yd[:, c].astype(F32)
        plane[160 * n : 160 * n + 160] = whole.astype(BF16)
    plane[800:1024] = jnp.zeros((224, 128), BF16)

    def quarter(k):
        return pl.ds(pl.multiple_of(k * 256, 256), 256)

    def slot(k):
        return pl.ds(pl.multiple_of(k * 32, 32), 32)

    crossing = []
    for s in range(1, 4):
        other, device = at_x(s)
        crossing.append(send(plane.at[quarter(other)], xin.at[s], x_s.at[s], x_r.at[s], device))
    gain(1)
    arrive(4, "sib")
    whole = plane[quarter(x)].astype(F32)
    for s in range(1, 4):
        crossing[s - 1].wait()
        whole = whole + xin[s].astype(F32)
    xsum[...] = whole.astype(BF16)
    along = []
    for s in range(1, 8):
        other, device = at_z(s)
        along.append(send(xsum.at[slot(other)], zin.at[s], z_s.at[s], z_r.at[s], device))
    gain(-2)
    whole = xsum[slot(z)].astype(F32)
    for s in range(1, 8):
        along[s - 1].wait()
        whole = whole + zin[s].astype(F32)
    zfull[slot(z)] = whole.astype(BF16)
    zback = []
    for s in range(1, 8):
        ref = zfull.at[slot(z)]
        zback.append(send(ref, ref, zb_s.at[s], zb_r.at[s], at_z(s)[1]))
    gain(2)
    for copy in zback:
        copy.wait()
    pfull[quarter(x)] = zfull[...]
    xback = []
    for s in range(1, 4):
        ref = pfull.at[quarter(x)]
        xback.append(send(ref, ref, xb_s.at[s], xb_r.at[s], at_x(s)[1]))
    gain(-3)
    gain(3)
    for copy in xback:
        copy.wait()
    for n in range(5):
        out_ref[part(core, y), 128 * n : 128 * n + 128] = pfull[160 * n : 160 * n + 160]

    def whole_part(k, send_sem, recv_sem, device):
        ref = out_ref.at[part(core, k)]
        return send(ref, ref, send_sem, recv_sem, device)

    def half_of(k, low_half):
        start = core * 640 + k * 160 + (0 if low_half else 80)
        return out_ref.at[pl.ds(pl.multiple_of(start, 16), 80)]

    def half_part(k, low_half, send_sem, recv_sem, device):
        ref = half_of(k, low_half)
        return send(ref, ref, send_sem, recv_sem, device)

    sent.append(whole_part(y, yb_s.at[0], yb_r.at[0], y_up[1]))
    sent.append(whole_part(y, yb_s.at[1], yb_r.at[1], y_down[1]))
    fin = [whole_part(y, fin_s.at[0], fin_r.at[0], sib)]
    gain(4)

    places = [(n, i, 192 * n + 16 * i) for n in range(5) for i in range(12)]
    small[180:192] = jnp.zeros((12, 640), F32)
    for c in range(2):
        for t in range(9):
            small[20 * t : 20 * t + 20] = prod[288 * c + 32 * t : 288 * c + 32 * t + 20]
        for n, i, f in places:
            piece = small[16 * i : 16 * i + 16, 128 * n : 128 * n + 128].astype(BF16)
            tb[c, f // 128, f % 128 : f % 128 + 16] = piece
        tb[c, 7, 64:128] = jnp.zeros((64, 128), BF16)
    there = []
    for s in range(1, 16):
        other, device = at_spot(s)
        there.append(send(tb.at[lax.rem(other, 2), other // 2], tin.at[s], t_s.at[s], t_r.at[s], device))
    tap(3)
    ref = out_ref.at[part(core, y_down[0])]
    remote(ref, ref, yb_s.at[0], yb_r.at[0], sib).wait_recv()
    ref = out_ref.at[part(core, y_up[0])]
    remote(ref, ref, yb_s.at[1], yb_r.at[1], sib).wait_recv()
    sent.append(half_part(y_down[0], True, yb_s.at[2], yb_r.at[2], y_up[1]))
    sent.append(half_part(y_up[0], False, yb_s.at[3], yb_r.at[3], y_down[1]))
    fin.append(whole_part(y_down[0], fin_s.at[1], fin_r.at[1], sib))
    fin.append(whole_part(y_up[0], fin_s.at[2], fin_r.at[2], sib))
    tap(4)
    tap(5)
    ref = half_of(far, True)
    remote(ref, ref, yb_s.at[2], yb_r.at[2], sib).wait_recv()
    ref = half_of(far, False)
    remote(ref, ref, yb_s.at[3], yb_r.at[3], sib).wait_recv()
    fin.append(whole_part(far, fin_s.at[3], fin_r.at[3], sib))
    tap(6)
    whole = tb[xlo, dp].astype(F32)
    for s in range(1, 16):
        there[s - 1].wait()
        whole = whole + tin[s].astype(F32)
    tfull[dp] = whole.astype(BF16)
    tback = []
    for s in range(1, 8):
        ref = tfull.at[dp]
        tback.append(send(ref, ref, u_s.at[s], u_r.at[s], at_dp(s)[1]))
    tap(7)
    tap(8)
    lat_ref[...] = acc[...].astype(BF16)
    for copy in tback:
        copy.wait()
    for n, i, f in places:
        small[16 * i : 16 * i + 16, 128 * n : 128 * n + 128] = tfull[f // 128, f % 128 : f % 128 + 16].astype(F32)
    for t in range(9):
        taps_ref[t] = small[20 * t : 20 * t + 20]
    for copy in fin:
        copy.wait()
    for copy in sent:
        copy.wait_send()


ATTEND = 52


def whole_kernel(*refs):
    hbm, (rows_ref, taps_ref, lat_ref), scratch = refs[:7], refs[7:10], refs[10:]
    shared, scratch = scratch[:11], scratch[11:]
    latent, cot, wq, wk, wv, wo, w, hidden, packed, lhs, parts = shared
    one, two, three = scratch[:15], scratch[15:15 + ATTEND], scratch[15 + ATTEND :]
    windows = first_kernel(hbm, latent, cot, wq, wk, wv, wo, w, hidden, packed, *one)
    attend_kernel(windows, lhs, packed, parts, *two)
    finish_kernel(parts, hidden, cot, wq, wk, wv, lhs, w, rows_ref, taps_ref, lat_ref, *three)


def whole(*args):
    dma = pltpu.SemaphoreType.DMA
    vmem = pl.BlockSpec(memory_space=pltpu.VMEM)

    def b16(*shape):
        return pltpu.VMEM(shape, BF16)

    def f32(*shape):
        return pltpu.VMEM(shape, F32)

    shared = [
        b16(128, 640), b16(128, 640), b16(320, 640), b16(320, 640), b16(320, 640), b16(320, 640),
        b16(9, 640, 640), b16(128, 640), b16(10, 128, 128), b16(8, 576, 256), b16(4, 128, 384),
    ]
    one = [
        dma((6,)), dma((9,)), b16(2, 64, 640), f32(656, 128), b16(16, 2, 32, 128), b16(18, 2, 32, 128),
        b16(3, 256, 640), f32(128, 640), f32(2, 128, 128),
        dma((2,)), dma((2,)), dma((16,)), dma((16,)), dma((16,)), dma((1,)),
    ]
    two = [
        b16(8, 640, 128), b16(8, 128, 640), b16(2, 512, 128), b16(512, 128), b16(512, 128), b16(512, 128), b16(512, 128),
        f32(64, 512), f32(64, 512),
        f32(8, 640, 512), f32(640, 512), b16(640, 512), b16(640, 512),
        f32(1, 512), f32(1, 512), f32(64, 512), f32(1, 512), f32(64, 512),
        f32(1, 512), f32(1, 512), f32(64, 512), f32(1, 512), f32(64, 512),
        f32(640, 128), b16(4, 640, 128), b16(4, 640, 128), b16(4, 640, 128), b16(4, 640, 128),
        f32(4, 72, 128), f32(4, 72, 128), f32(4, 8, 128), f32(128, 128), b16(3, 512, 128), b16(4, 3, 128, 128),
        dma((4,)), dma((4,)), dma((2, 4)), dma((2, 4)),
        dma((4,)), dma((4,)), dma((4,)), dma((4,)), dma((4,)), dma((4,)), dma((4,)), dma((4,)),
        dma((4,)), dma((4,)), dma((4,)), dma((4,)), dma((2, 4)), dma((2, 4)),
    ]
    three = [
        b16(8, 256, 640), b16(2, 64, 640), b16(3, 256, 640), f32(128, 640),
        f32(576, 640), f32(192, 640), b16(384, 128),
        b16(1280, 640), b16(4, 160, 640), b16(80, 640), b16(80, 640), b16(160, 640), b16(160, 640),
        b16(1024, 128), b16(4, 256, 128), b16(256, 128), b16(8, 32, 128), b16(256, 128), b16(1024, 128),
        b16(2, 8, 128, 128), b16(16, 128, 128), b16(8, 128, 128),
        dma((2,)), dma((2,)), dma((4,)), dma((4,)), dma((8,)), dma((10,)), dma((8,)),
        dma((4,)), dma((4,)), dma((4,)), dma((4,)), dma((4,)), dma((4,)), dma((8,)), dma((8,)),
        dma((8,)), dma((8,)), dma((4,)), dma((4,)), dma((4,)), dma((4,)), dma((4,)), dma((4,)),
        dma((16,)), dma((16,)), dma((8,)), dma((8,)),
    ]
    return pl.pallas_call(
        whole_kernel,
        out_shape=(
            jax.ShapeDtypeStruct((1280, 640), BF16),
            jax.ShapeDtypeStruct((9, 20, 640), F32),
            jax.ShapeDtypeStruct((128, 640), BF16),
        ),
        in_specs=[pl.BlockSpec(memory_space=pl.ANY)] * 7,
        out_specs=(vmem,) * 3,
        scratch_shapes=shared + one + two + three,
        compiler_params=pltpu.CompilerParams(
            collective_id=0, has_side_effects=True, vmem_limit_bytes=60 * 1024 * 1024
        ),
        name="whole",
    )(*args)


def hand_kernel(rows_ref, taps_ref, lat_ref, taps_out, lat_out, *rest):
    outs, (rows, wide, in_sem, out_sem) = rest[:4], rest[4:]
    direct = [
        pltpu.make_async_copy(taps_ref, taps_out, out_sem.at[4]),
        pltpu.make_async_copy(lat_ref, lat_out, out_sem.at[5]),
    ]
    loads = [
        pltpu.make_async_copy(rows_ref.at[AW * i : AW * i + AW], rows.at[i], in_sem.at[i]) for i in range(4)
    ]
    for copy in loads + direct:
        copy.start()
    stores = []
    for i in range(4):
        loads[i].wait()
        wide[i] = rows[i].astype(F32)
        copy = pltpu.make_async_copy(wide.at[i], outs[i], out_sem.at[i])
        copy.start()
        stores.append(copy)
    for copy in stores + direct:
        copy.wait()


def hand_out(rows, taps, grad_latent):
    anywhere = pl.BlockSpec(memory_space=pl.ANY)
    return pl.pallas_call(
        hand_kernel,
        out_shape=(
            jax.ShapeDtypeStruct(taps.shape, F32),
            jax.ShapeDtypeStruct(grad_latent.shape, BF16),
        )
        + (jax.ShapeDtypeStruct((AW, 640), F32),) * 4,
        in_specs=[anywhere] * 3,
        out_specs=(anywhere,) * 6,
        scratch_shapes=[
            pltpu.VMEM((4, AW, 640), BF16),
            pltpu.VMEM((4, AW, 640), F32),
            pltpu.SemaphoreType.DMA((4,)),
            pltpu.SemaphoreType.DMA((6,)),
        ],
        compiler_params=pltpu.CompilerParams(vmem_limit_bytes=60 * 1024 * 1024),
        name="hand_out",
    )(rows, taps, grad_latent)


def body(latent, cotangent, conv_weight, query_weight, key_weight, value_weight, out_weight):
    sums = whole(
        latent.reshape(128, 640), cotangent.reshape(128, 640), out_weight, key_weight.T, value_weight.T,
        query_weight.T, conv_weight.reshape(9, 640, 640),
    )
    taps, grad_latent, query, key, value, out = hand_out(*sums)
    return (grad_latent.reshape(latent.shape), taps.reshape(3, 3, 20, 640), query.T, key.T, value.T, out)


def solution(mesh):
    placed = (P("dp", "patch", None, None), P("dp", "patch", None, None), P(), P(), P(), P(), P())
    return jax.shard_map(
        body,
        mesh=mesh,
        in_specs=placed,
        out_specs=(P("dp", "patch", None, None), P(None, None, "patch", None), P(), P(), P(), P()),
        check_vma=False,
    )
```

time: 181 us -> 161 us (0.89)
  local copies, waits for them, and re-layouts: 10.3 us -> 0 us
  Pallas kernels: 167 us -> 160 us
  other arithmetic: 2.48 us -> 0 us
    unnamed x23 -> x0, local copies, waits for them, and re-layouts: 9.1 us -> none
    pallas_call x3 -> x2, Pallas kernels: 167 us -> 160 us  [the longest x1 137 us: whole(): pl.pallas_call(whole_kernel, out_shape=(jax.ShapeDtypeStruct((1280, 640),...]
    convert_element_type x4 -> x0, other arithmetic: 2.48 us -> none  [the longest x1 1.43 us: body(): rows[:640, 320:].astype(F32)]
where the time goes in v2:
time: 161 us; the launch traced here: 160 us
  Pallas kernels  160 us (99%)
    pallas_call x1, Pallas kernels, whole(): pl.pallas_call(whole_kernel, out_shape=(jax.ShapeDtypeStruct((1280, 640),...  137 us
    pallas_call x1, Pallas kernels, hand_out(): pl.pallas_call(hand_kernel, out_shape=(jax.ShapeDtypeStruct(taps.shape, F...  22.9 us

profile of v2, /device:TPU:8, one launch (start us, length us, event | category | flops | bytes accessed | tf_op | source)
XLA Modules:
  0.0 160.5 jit_solution(17368223932616042225)
XLA Ops:
  0.6 136.8 %whole.1 = (bf16[1280,640]{1,0:T(8,128)(2,1)}, f32[9,20,640]{2,1,0:T(8,128)}, bf16[128,640]{1,0:T(8,128)(2,1)}) custom-call(bf16[128,640]{1,0:T(8,128)(2,1)} %bitcast.15, bf16[128,640]{1,0:T(8,128)(2,1)} %bitcast.16, bf16[320,640]{1,0:T(8,128)(2,1)} %refs_2_.1, bf16[320,640]{1,0:T(8,128)(2,1)} %bitcast.12, bf16[320,640]{1,0:T(8,128)(2,1)} %bitcast.13, ...), custom_call_target="tpu_custom_call" | custom-call | tf_op jit(solution)/shard_map/whole/pallas_call | solution.py:814
  137.4 22.9 %hand_out.1 = (f32[9,20,640]{2,1,0:T(8,128)}, bf16[128,640]{1,0:T(8,128)(2,1)}, f32[320,640]{1,0:T(8,128)}, f32[320,640]{1,0:T(8,128)}, f32[320,640]{1,0:T(8,128)}, /*index=5*/f32[320,640]{1,0:T(8,128)}) custom-call(bf16[1280,640]{1,0:T(8,128)(2,1)} %get-tuple-element.15.rows_ref, f32[9,20,640]{2,1,0:T(8,128)} %get-tuple-element.16.taps_ref, ...), custom_call_target="tpu_custom_call" | custom-call | tf_op jit(solution)/shard_map/hand_out/pallas_call | solution.py:855

commit v3 on v2

--- a/solution.py
+++ b/solution.py
@@ -121,9 +121,6 @@
             def _():
                 ring_up(s).wait_recv()
                 ring_up(s + 1).start()
-
-            @pl.when(t == 2 * s + 2)
-            def _():
                 ring_down(s).wait_recv()
                 ring_down(s + 1).start()
 
@@ -480,7 +477,7 @@
 
 
 def finish_kernel(parts_ref, hid_ref, cot_ref, wq_ref, wk_ref, wv_ref, lhs_ref, w, out_ref, taps_ref, lat_ref,
-                  gh, halo, sh, acc, prod, small, turned, xs, half, ya, yb, yc, yd,
+                  gh, halo, sh, acc, prod, small, turned, xs, half, ra, rb, rc, rd,
                   plane, xin, xsum, zin, zfull, pfull, tb, tin, tfull, halo_s, halo_r, up_s, down_s, sib_s, own_r, sib_r,
                   pair_s, pair_r, y_s, y_r, x_s, x_r, z_s, z_r, zb_s, zb_r, xb_s, xb_r, yb_s, yb_r, fin_s, fin_r,
                   t_s, t_r, u_s, u_r):
@@ -499,7 +496,7 @@
         return other, (xhi * 4 + other, p)
 
     def at_x(s):
-        other = lax.rem(x + s, 4)
+        other = lax.rem(x + s + 4, 4)
         return other, (other // 2 * 4 + y, lax.rem(other, 2) * 16 + z * 2 + core)
 
     spot = dp * 2 + xlo
@@ -568,10 +565,24 @@
         right = hid_ref if t else cot_ref
         xs[AW * i : AW * i + AW] = jnp.dot(turned[0:AW], right[...], preferred_element_type=F32).astype(BF16)
 
-    def part(c, k):
-        return pl.ds(pl.multiple_of(c * 640 + k * 160, 16), 160)
-
-    pair = [send(xs.at[part(1 - core, k)], half.at[k], pair_s.at[k], pair_r.at[k], sib) for k in range(4)]
+    first_at, second_at = (at_y, at_x), (at_x, at_y)
+    first_index, second_index = (y, x), (x, y)
+    halves = range(2)
+
+    def part(c, h, k):
+        return pl.ds(pl.multiple_of(c * 640 + h * 320 + k * 80, 16), 80)
+
+    def low_of(c, h, k):
+        return pl.ds(pl.multiple_of(c * 640 + h * 320 + k * 80, 16), 48)
+
+    def high_of(c, h, k):
+        return pl.ds(pl.multiple_of(c * 640 + h * 320 + k * 80 + 48, 16), 32)
+
+    pair = []
+    for h in halves:
+        theirs = pl.ds(pl.multiple_of((1 - core) * 640 + h * 320, 16), 320)
+        there = pl.ds(320 * h, 320)
+        pair.append(send(xs.at[theirs], half.at[there], pair_s.at[h], pair_r.at[h], sib))
     arrive(-1, "up", "sib")
     arrive(1, "down", "sib")
 
@@ -611,95 +622,103 @@
     tap(0)
     for copy in pair:
         copy.wait()
-    for k in range(4):
-        half[k] = (half[k].astype(F32) + xs[part(core, k)].astype(F32)).astype(BF16)
-    far = lax.rem(y + 2, 4)
-    y_up, y_down = at_y(1), at_y(-1)
-    sent.append(send(half.at[far, 0:80], ya, y_s.at[0], y_r.at[0], y_up[1]))
-    sent.append(send(half.at[far, 80:160], yb, y_s.at[1], y_r.at[1], y_down[1]))
+    for h in halves:
+        mine_rows = pl.ds(pl.multiple_of(core * 640 + h * 320, 16), 320)
+        r = slice(320 * h, 320 * h + 320)
+        half[r] = (half[r].astype(F32) + xs[mine_rows].astype(F32)).astype(BF16)
+    up, down, far = [], [], []
+    for h in halves:
+        up.append(first_at[h](1))
+        down.append(first_at[h](-1))
+        far.append(lax.rem(first_index[h] + 2, 4))
+        sent.append(send(half.at[low_of(0, h, far[h])], ra.at[h], y_s.at[h, 0], y_r.at[h, 0], up[h][1]))
+        sent.append(send(half.at[high_of(0, h, far[h])], rb.at[h], y_s.at[h, 1], y_r.at[h, 1], down[h][1]))
     tap(1)
     arrive(-2, "up", "sib")
     arrive(2, "down", "sib")
-    remote(half.at[far, 0:80], ya, y_s.at[0], y_r.at[0], sib).wait_recv()
-    remote(half.at[far, 80:160], yb, y_s.at[1], y_r.at[1], sib).wait_recv()
-    half[y_up[0], 0:80] = (half[y_up[0], 0:80].astype(F32) + ya[...].astype(F32)).astype(BF16)
-    half[y_down[0], 80:160] = (half[y_down[0], 80:160].astype(F32) + yb[...].astype(F32)).astype(BF16)
-    sent.append(send(half.at[y_up[0]], yc, y_s.at[2], y_r.at[2], y_up[1]))
-    sent.append(send(half.at[y_down[0]], yd, y_s.at[3], y_r.at[3], y_down[1]))
+    for h in halves:
+        remote(half.at[low_of(0, h, 0)], ra.at[h], y_s.at[h, 0], y_r.at[h, 0], sib).wait_recv()
+        remote(half.at[high_of(0, h, 0)], rb.at[h], y_s.at[h, 1], y_r.at[h, 1], sib).wait_recv()
+        r = low_of(0, h, up[h][0])
+        half[r] = (half[r].astype(F32) + ra[h].astype(F32)).astype(BF16)
+        r = high_of(0, h, down[h][0])
+        half[r] = (half[r].astype(F32) + rb[h].astype(F32)).astype(BF16)
+        sent.append(send(half.at[part(0, h, up[h][0])], rc.at[h], y_s.at[h, 2], y_r.at[h, 2], up[h][1]))
+        sent.append(send(half.at[part(0, h, down[h][0])], rd.at[h], y_s.at[h, 3], y_r.at[h, 3], down[h][1]))
     tap(2)
     gain(0, True)
     arrive(-3, "up", "sib")
     arrive(3, "down", "sib")
     gain(-1)
-    remote(half.at[0], yc, y_s.at[2], y_r.at[2], sib).wait_recv()
-    remote(half.at[0], yd, y_s.at[3], y_r.at[3], sib).wait_recv()
-    for n in range(5):
-        c = slice(128 * n, 128 * n + 128)
-        whole = half[y, :, c].astype(F32) + yc[:, c].astype(F32) + yd[:, c].astype(F32)
-        plane[160 * n : 160 * n + 160] = whole.astype(BF16)
-    plane[800:1024] = jnp.zeros((224, 128), BF16)
-
     def quarter(k):
-        return pl.ds(pl.multiple_of(k * 256, 256), 256)
+        return pl.ds(pl.multiple_of(k * 128, 128), 128)
 
     def slot(k):
-        return pl.ds(pl.multiple_of(k * 32, 32), 32)
+        return pl.ds(pl.multiple_of(k * 16, 16), 16)
 
     crossing = []
-    for s in range(1, 4):
-        other, device = at_x(s)
-        crossing.append(send(plane.at[quarter(other)], xin.at[s], x_s.at[s], x_r.at[s], device))
+    for h in halves:
+        remote(half.at[part(0, h, 0)], rc.at[h], y_s.at[h, 2], y_r.at[h, 2], sib).wait_recv()
+        remote(half.at[part(0, h, 0)], rd.at[h], y_s.at[h, 3], y_r.at[h, 3], sib).wait_recv()
+        whole = half[part(0, h, first_index[h])].astype(F32) + rc[h].astype(F32) + rd[h].astype(F32)
+        for n in range(5):
+            plane[h, 80 * n : 80 * n + 80] = whole[:, 128 * n : 128 * n + 128].astype(BF16)
+        plane[h, 400:512] = jnp.zeros((112, 128), BF16)
+        for s in range(1, 4):
+            other, device = second_at[h](s)
+            crossing.append(send(plane.at[h, quarter(other)], xin.at[h, s], x_s.at[h, s], x_r.at[h, s], device))
     gain(1)
     arrive(4, "sib")
-    whole = plane[quarter(x)].astype(F32)
-    for s in range(1, 4):
-        crossing[s - 1].wait()
-        whole = whole + xin[s].astype(F32)
-    xsum[...] = whole.astype(BF16)
+    for copy in crossing:
+        copy.wait()
+    for h in halves:
+        whole = plane[h, quarter(second_index[h])].astype(F32)
+        for s in range(1, 4):
+            whole = whole + xin[h, s].astype(F32)
+        xsum[h] = whole.astype(BF16)
     along = []
     for s in range(1, 8):
         other, device = at_z(s)
-        along.append(send(xsum.at[slot(other)], zin.at[s], z_s.at[s], z_r.at[s], device))
+        along.append(send(xsum.at[:, slot(other), :], zin.at[s], z_s.at[s], z_r.at[s], device))
     gain(-2)
-    whole = xsum[slot(z)].astype(F32)
+    whole = xsum[:, slot(z), :].astype(F32)
     for s in range(1, 8):
         along[s - 1].wait()
         whole = whole + zin[s].astype(F32)
-    zfull[slot(z)] = whole.astype(BF16)
+    zfull[:, slot(z), :] = whole.astype(BF16)
     zback = []
     for s in range(1, 8):
-        ref = zfull.at[slot(z)]
+        ref = zfull.at[:, slot(z), :]
         zback.append(send(ref, ref, zb_s.at[s], zb_r.at[s], at_z(s)[1]))
     gain(2)
     for copy in zback:
         copy.wait()
-    pfull[quarter(x)] = zfull[...]
     xback = []
-    for s in range(1, 4):
-        ref = pfull.at[quarter(x)]
-        xback.append(send(ref, ref, xb_s.at[s], xb_r.at[s], at_x(s)[1]))
+    for h in halves:
+        pfull[h, quarter(second_index[h])] = zfull[h]
+        for s in range(1, 4):
+            ref = pfull.at[h, quarter(second_index[h])]
+            xback.append(send(ref, ref, xb_s.at[h, s], xb_r.at[h, s], second_at[h](s)[1]))
     gain(-3)
     gain(3)
     for copy in xback:
         copy.wait()
-    for n in range(5):
-        out_ref[part(core, y), 128 * n : 128 * n + 128] = pfull[160 * n : 160 * n + 160]
-
-    def whole_part(k, send_sem, recv_sem, device):
-        ref = out_ref.at[part(core, k)]
-        return send(ref, ref, send_sem, recv_sem, device)
-
-    def half_of(k, low_half):
-        start = core * 640 + k * 160 + (0 if low_half else 80)
-        return out_ref.at[pl.ds(pl.multiple_of(start, 16), 80)]
-
-    def half_part(k, low_half, send_sem, recv_sem, device):
-        ref = half_of(k, low_half)
-        return send(ref, ref, send_sem, recv_sem, device)
-
-    sent.append(whole_part(y, yb_s.at[0], yb_r.at[0], y_up[1]))
-    sent.append(whole_part(y, yb_s.at[1], yb_r.at[1], y_down[1]))
-    fin = [whole_part(y, fin_s.at[0], fin_r.at[0], sib)]
+    fin = []
+    for h in halves:
+        for n in range(5):
+            out_ref[part(core, h, first_index[h]), 128 * n : 128 * n + 128] = pfull[h, 80 * n : 80 * n + 80]
+
+    def forward(rows, send_sem, recv_sem, device):
+        return send(out_ref.at[rows], out_ref.at[rows], send_sem, recv_sem, device)
+
+    def landed(rows, h, i):
+        remote(out_ref.at[rows], out_ref.at[rows], yb_s.at[h, i], yb_r.at[h, i], sib).wait_recv()
+
+    for h in halves:
+        rows = part(core, h, first_index[h])
+        sent.append(forward(rows, yb_s.at[h, 0], yb_r.at[h, 0], up[h][1]))
+        sent.append(forward(rows, yb_s.at[h, 1], yb_r.at[h, 1], down[h][1]))
+        fin.append(forward(rows, fin_s.at[h, 0], fin_r.at[h, 0], sib))
     gain(4)
 
     places = [(n, i, 192 * n + 16 * i) for n in range(5) for i in range(12)]
@@ -716,21 +735,19 @@
         other, device = at_spot(s)
         there.append(send(tb.at[lax.rem(other, 2), other // 2], tin.at[s], t_s.at[s], t_r.at[s], device))
     tap(3)
-    ref = out_ref.at[part(core, y_down[0])]
-    remote(ref, ref, yb_s.at[0], yb_r.at[0], sib).wait_recv()
-    ref = out_ref.at[part(core, y_up[0])]
-    remote(ref, ref, yb_s.at[1], yb_r.at[1], sib).wait_recv()
-    sent.append(half_part(y_down[0], True, yb_s.at[2], yb_r.at[2], y_up[1]))
-    sent.append(half_part(y_up[0], False, yb_s.at[3], yb_r.at[3], y_down[1]))
-    fin.append(whole_part(y_down[0], fin_s.at[1], fin_r.at[1], sib))
-    fin.append(whole_part(y_up[0], fin_s.at[2], fin_r.at[2], sib))
+    for h in halves:
+        landed(part(core, h, down[h][0]), h, 0)
+        landed(part(core, h, up[h][0]), h, 1)
+        sent.append(forward(low_of(core, h, down[h][0]), yb_s.at[h, 2], yb_r.at[h, 2], up[h][1]))
+        sent.append(forward(high_of(core, h, up[h][0]), yb_s.at[h, 3], yb_r.at[h, 3], down[h][1]))
+        fin.append(forward(part(core, h, down[h][0]), fin_s.at[h, 1], fin_r.at[h, 1], sib))
+        fin.append(forward(part(core, h, up[h][0]), fin_s.at[h, 2], fin_r.at[h, 2], sib))
     tap(4)
     tap(5)
-    ref = half_of(far, True)
-    remote(ref, ref, yb_s.at[2], yb_r.at[2], sib).wait_recv()
-    ref = half_of(far, False)
-    remote(ref, ref, yb_s.at[3], yb_r.at[3], sib).wait_recv()
-    fin.append(whole_part(far, fin_s.at[3], fin_r.at[3], sib))
+    for h in halves:
+        landed(low_of(core, h, far[h]), h, 2)
+        landed(high_of(core, h, far[h]), h, 3)
+        fin.append(forward(part(core, h, far[h]), fin_s.at[h, 3], fin_r.at[h, 3], sib))
     tap(6)
     whole = tb[xlo, dp].astype(F32)
     for s in range(1, 16):
@@ -803,12 +820,12 @@
     three = [
         b16(8, 256, 640), b16(2, 64, 640), b16(3, 256, 640), f32(128, 640),
         f32(576, 640), f32(192, 640), b16(384, 128),
-        b16(1280, 640), b16(4, 160, 640), b16(80, 640), b16(80, 640), b16(160, 640), b16(160, 640),
-        b16(1024, 128), b16(4, 256, 128), b16(256, 128), b16(8, 32, 128), b16(256, 128), b16(1024, 128),
+        b16(1280, 640), b16(640, 640), b16(2, 48, 640), b16(2, 32, 640), b16(2, 80, 640), b16(2, 80, 640),
+        b16(2, 512, 128), b16(2, 4, 128, 128), b16(2, 128, 128), b16(8, 2, 16, 128), b16(2, 128, 128), b16(2, 512, 128),
         b16(2, 8, 128, 128), b16(16, 128, 128), b16(8, 128, 128),
         dma((2,)), dma((2,)), dma((4,)), dma((4,)), dma((8,)), dma((10,)), dma((8,)),
-        dma((4,)), dma((4,)), dma((4,)), dma((4,)), dma((4,)), dma((4,)), dma((8,)), dma((8,)),
-        dma((8,)), dma((8,)), dma((4,)), dma((4,)), dma((4,)), dma((4,)), dma((4,)), dma((4,)),
+        dma((2,)), dma((2,)), dma((2, 4)), dma((2, 4)), dma((2, 4)), dma((2, 4)), dma((8,)), dma((8,)),
+        dma((8,)), dma((8,)), dma((2, 4)), dma((2, 4)), dma((2, 4)), dma((2, 4)), dma((2, 4)), dma((2, 4)),
         dma((16,)), dma((16,)), dma((8,)), dma((8,)),
     ]
     return pl.pallas_call(
@@ -829,24 +846,27 @@
 
 
 def hand_kernel(rows_ref, taps_ref, lat_ref, taps_out, lat_out, *rest):
-    outs, (rows, wide, in_sem, out_sem) = rest[:4], rest[4:]
-    direct = [
-        pltpu.make_async_copy(taps_ref, taps_out, out_sem.at[4]),
-        pltpu.make_async_copy(lat_ref, lat_out, out_sem.at[5]),
-    ]
+    outs, (rows, wide, taps, lat, in_sem, out_sem) = rest[:4], rest[4:]
     loads = [
         pltpu.make_async_copy(rows_ref.at[AW * i : AW * i + AW], rows.at[i], in_sem.at[i]) for i in range(4)
     ]
-    for copy in loads + direct:
+    loads.append(pltpu.make_async_copy(taps_ref, taps, in_sem.at[4]))
+    loads.append(pltpu.make_async_copy(lat_ref, lat, in_sem.at[5]))
+    for copy in loads:
         copy.start()
     stores = []
-    for i in range(4):
+    for i in range(6):
         loads[i].wait()
-        wide[i] = rows[i].astype(F32)
-        copy = pltpu.make_async_copy(wide.at[i], outs[i], out_sem.at[i])
+        if i < 4:
+            wide[i] = rows[i].astype(F32)
+            copy = pltpu.make_async_copy(wide.at[i], outs[i], out_sem.at[i])
+        elif i == 4:
+            copy = pltpu.make_async_copy(taps, taps_out, out_sem.at[i])
+        else:
+            copy = pltpu.make_async_copy(lat, lat_out, out_sem.at[i])
         copy.start()
         stores.append(copy)
-    for copy in stores + direct:
+    for copy in stores:
         copy.wait()
 
 
@@ -864,7 +884,9 @@
         scratch_shapes=[
             pltpu.VMEM((4, AW, 640), BF16),
             pltpu.VMEM((4, AW, 640), F32),
-            pltpu.SemaphoreType.DMA((4,)),
+            pltpu.VMEM(taps.shape, F32),
+            pltpu.VMEM(grad_latent.shape, BF16),
+            pltpu.SemaphoreType.DMA((6,)),
             pltpu.SemaphoreType.DMA((6,)),
         ],
         compiler_params=pltpu.CompilerParams(vmem_limit_bytes=60 * 1024 * 1024),

time: 161 us -> 135 us (0.84)
  Pallas kernels: 160 us -> 133 us
    pallas_call x1, Pallas kernels: 22.9 us -> 3.09 us  [hand_out(): pl.pallas_call(hand_kernel, out_shape=(jax.ShapeDtypeStruct(taps.shape, F...]
    pallas_call x1, Pallas kernels: 137 us -> 130 us  [whole(): pl.pallas_call(whole_kernel, out_shape=(jax.ShapeDtypeStruct((1280, 640),...]
where the time goes in v3:
time: 135 us; the launch traced here: 134 us
  Pallas kernels  133 us (99%)
    pallas_call x1, Pallas kernels, whole(): pl.pallas_call(whole_kernel, out_shape=(jax.ShapeDtypeStruct((1280, 640),...  130 us
    pallas_call x1, Pallas kernels, hand_out(): pl.pallas_call(hand_kernel, out_shape=(jax.ShapeDtypeStruct(taps.shape, F...  3.09 us

profile of v3, /device:TPU:8, one launch (start us, length us, event | category | flops | bytes accessed | tf_op | source)
XLA Modules:
  0.0 134.2 jit_solution(15943750829218707484)
XLA Ops:
  0.6 130.3 %whole.1 = (bf16[1280,640]{1,0:T(8,128)(2,1)}, f32[9,20,640]{2,1,0:T(8,128)}, bf16[128,640]{1,0:T(8,128)(2,1)}) custom-call(bf16[128,640]{1,0:T(8,128)(2,1)} %bitcast.15, bf16[128,640]{1,0:T(8,128)(2,1)} %bitcast.16, bf16[320,640]{1,0:T(8,128)(2,1)} %refs_2_.1, bf16[320,640]{1,0:T(8,128)(2,1)} %bitcast.12, bf16[320,640]{1,0:T(8,128)(2,1)} %bitcast.13, ...), custom_call_target="tpu_custom_call" | custom-call | tf_op jit(solution)/shard_map/whole/pallas_call | solution.py:831
  130.9 3.1 %hand_out.1 = (f32[9,20,640]{2,1,0:T(8,128)}, bf16[128,640]{1,0:T(8,128)(2,1)}, f32[320,640]{1,0:T(8,128)}, f32[320,640]{1,0:T(8,128)}, f32[320,640]{1,0:T(8,128)}, /*index=5*/f32[320,640]{1,0:T(8,128)}) custom-call(bf16[1280,640]{1,0:T(8,128)(2,1)} %get-tuple-element.15.rows_ref, f32[9,20,640]{2,1,0:T(8,128)} %get-tuple-element.16.taps_ref, ...), custom_call_target="tpu_custom_call" | custom-call | tf_op jit(solution)/shard_map/hand_out/pallas_call | solution.py:875

commit v4 on v3

--- a/solution.py
+++ b/solution.py
@@ -76,20 +76,21 @@
     for ref in (low, low4, att, att4, dq, dq4):
         ref[...] = jnp.zeros(ref.shape, F32)
 
-    def ring_up(s):
-        k = lax.rem(z + 8 - s, 8)
-        ref = kv.at[k] if s < 3 else kv.at[k, 0:320]
-        return remote(ref, ref, up_s.at[s], up_r.at[s], at_z(1))
-
-    def ring_down(s):
-        k = lax.rem(z + s, 8)
-        ref = kv.at[k] if s < 3 else kv.at[k, 320:640]
-        return remote(ref, ref, down_s.at[s], down_r.at[s], at_z(-1))
+    cuts = (slice(0, 320), slice(320, 640))
+
+    def ring_up(s, i):
+        ref = kv.at[lax.rem(z + 8 - s, 8), cuts[i]]
+        return remote(ref, ref, up_s.at[s, i], up_r.at[s, i], at_z(1))
+
+    def ring_down(s, i):
+        ref = kv.at[lax.rem(z + s, 8), cuts[i]]
+        return remote(ref, ref, down_s.at[s, i], down_r.at[s, i], at_z(-1))
 
     for copy in first:
         copy.wait()
-    ring_up(0).start()
-    ring_down(0).start()
+    for i in range(2):
+        ring_up(0, i).start()
+        ring_down(0, i).start()
     windows(lhs_ref)
     for copy in second:
         copy.wait()
@@ -119,15 +120,18 @@
         for s in range(3):
             @pl.when(t == 2 * s + 1)
             def _():
-                ring_up(s).wait_recv()
-                ring_up(s + 1).start()
-                ring_down(s).wait_recv()
-                ring_down(s + 1).start()
+                for i in range(2):
+                    ring_up(s, i).wait_recv()
+                    if s < 2 or i == 0:
+                        ring_up(s + 1, i).start()
+                    ring_down(s, i).wait_recv()
+                    if s < 2 or i == 1:
+                        ring_down(s + 1, i).start()
 
         @pl.when(t == 7)
         def _():
-            ring_up(3).wait_recv()
-            ring_down(3).wait_recv()
+            ring_up(3, 0).wait_recv()
+            ring_down(3, 1).wait_recv()
 
         offset = jnp.where(lax.rem(t, 2) == 1, 8 - (t + 1) // 2, t // 2)
         b = lax.rem(z + offset, 8)
@@ -162,6 +166,12 @@
     def stat_copy(s):
         return remote(stat.at[j], stat.at[j], stat_s.at[s], stat_r.at[s], in_quad(s)[1])
 
+    late = []
+    for q in quarters:
+        stage[1, q] = jnp.concatenate([att[:, q], jnp.zeros((64, 128), F32)], axis=0).T.astype(BF16)
+    for s in range(1, 4):
+        m, device = in_quad(s)
+        late.append(send(stage.at[1, rows(m), :], res.at[j, 1], g_s.at[2, s], g_r.at[2, s], device))
     for copy in mixing:
         copy.wait()
     tops = [mix_in[s, 64:65] for s in range(4)]
@@ -180,13 +190,19 @@
     for s in range(1, 4):
         stat_copy(s).start()
 
-    def sum_up(s):
-        r = slice(0, 320) if s == 0 else slice(0, 640)
-        return remote(box_up.at[s, r], ahead.at[s, r], rup_s.at[s], rup_r.at[s], at_z(1))
-
-    def sum_down(s):
-        r = slice(320, 640) if s == 0 else slice(0, 640)
-        return remote(box_down.at[s, r], behind.at[s, r], rdown_s.at[s], rdown_r.at[s], at_z(-1))
+    def sum_up(s, i):
+        return remote(box_up.at[s, cuts[i]], ahead.at[s, cuts[i]], rup_s.at[s, i], rup_r.at[s, i], at_z(1))
+
+    def sum_down(s, i):
+        return remote(
+            box_down.at[s, cuts[i]], behind.at[s, cuts[i]], rdown_s.at[s, i], rdown_r.at[s, i], at_z(-1)
+        )
+
+    def pass_on(box, landed, step, s, i):
+        c = cuts[i]
+        step(s, i).wait_recv()
+        box[s + 1, c] = (part[c] + landed[s, c].astype(F32)).astype(BF16)
+        step(s + 1, i).start()
 
     def slopes(b, keys, q, top, delta):
         p = jnp.exp2(scores[b, keys, q] - top[:, q])
@@ -222,52 +238,46 @@
 
         @pl.when(t == 0)
         def _():
-            box_up[0, 0:320] = part[0:320].astype(BF16)
-            sum_up(0).start()
-            box_down[0, 320:640] = part[320:640].astype(BF16)
-            sum_down(0).start()
+            box_up[0, cuts[0]] = part[cuts[0]].astype(BF16)
+            sum_up(0, 0).start()
+            box_down[0, cuts[1]] = part[cuts[1]].astype(BF16)
+            sum_down(0, 1).start()
 
         @pl.when(t == 1)
         def _():
-            sum_up(0).wait_recv()
-            box_up[1, 0:320] = (part[0:320] + ahead[0, 0:320].astype(F32)).astype(BF16)
-            box_up[1, 320:640] = part[320:640].astype(BF16)
-            sum_up(1).start()
+            box_up[1, cuts[1]] = part[cuts[1]].astype(BF16)
+            sum_up(1, 1).start()
+            pass_on(box_up, ahead, sum_up, 0, 0)
 
         @pl.when(t == 2)
         def _():
-            sum_down(0).wait_recv()
-            box_down[1, 0:320] = part[0:320].astype(BF16)
-            box_down[1, 320:640] = (part[320:640] + behind[0, 320:640].astype(F32)).astype(BF16)
-            sum_down(1).start()
+            box_down[1, cuts[0]] = part[cuts[0]].astype(BF16)
+            sum_down(1, 0).start()
+            pass_on(box_down, behind, sum_down, 0, 1)
 
         for s in range(1, 3):
             @pl.when(t == 2 * s + 1)
             def _():
-                sum_up(s).wait_recv()
-                box_up[s + 1] = (part[...] + ahead[s].astype(F32)).astype(BF16)
-                sum_up(s + 1).start()
+                pass_on(box_up, ahead, sum_up, s, 1)
+                pass_on(box_up, ahead, sum_up, s, 0)
 
             @pl.when(t == 2 * s + 2)
             def _():
-                sum_down(s).wait_recv()
-                box_down[s + 1] = (part[...] + behind[s].astype(F32)).astype(BF16)
-                sum_down(s + 1).start()
+                pass_on(box_down, behind, sum_down, s, 0)
+                pass_on(box_down, behind, sum_down, s, 1)
 
         return carry
 
     lax.fori_loop(0, 8, pass_two, 0)
     for q in quarters:
-        both = jnp.concatenate([dq[:, q] * HD ** -0.5, att[:, q]], axis=0)
+        both = jnp.concatenate([dq[:, q], dq4[:, q]], axis=0) * HD ** -0.5
         stage[0, q] = both.T.astype(BF16)
-        both = jnp.concatenate([dq4[:, q] * HD ** -0.5, jnp.zeros((64, 128), F32)], axis=0)
-        stage[1, q] = both.T.astype(BF16)
-    late = []
     for s in range(1, 4):
         m, device = in_quad(s)
-        late.append(send(stage.at[0:2, rows(m), :], res.at[j, 0:2], g_s.at[0, s], g_r.at[0, s], device))
-    sum_up(3).wait_recv()
-    sum_down(3).wait_recv()
+        late.append(send(stage.at[0, rows(m), :], res.at[j, 0], g_s.at[0, s], g_r.at[0, s], device))
+    for i in range(2):
+        sum_up(3, i).wait_recv()
+        sum_down(3, i).wait_recv()
     stage[2] = (part[main] + ahead[3, main].astype(F32) + behind[3, main].astype(F32)).astype(BF16)
     for s in range(1, 4):
         m, device = in_quad(s)
@@ -276,24 +286,29 @@
     for t in range(3):
         res[j, t] = stage[t, rows(j), :]
     for s in range(4):
-        ring_up(s).wait_send()
-        ring_down(s).wait_send()
-        sum_up(s).wait_send()
-        sum_down(s).wait_send()
+        for i in range(2):
+            if s < 3 or i == 0:
+                ring_up(s, i).wait_send()
+            if s < 3 or i == 1:
+                ring_down(s, i).wait_send()
+            if s > 0 or i == 0:
+                sum_up(s, i).wait_send()
+            if s > 0 or i == 1:
+                sum_down(s, i).wait_send()
     for copy in late:
         copy.wait()
 
     def swap(a):
         return pltpu.roll(a, 64, axis=1)
 
-    for t, source, high in ((0, 0, True), (1, 0, False), (2, 2, False), (3, 2, True)):
+    for t, source, high in ((0, 1, False), (1, 0, False), (2, 2, False), (3, 2, True)):
         for i in range(2):
             a, b = res[2 * i, source].astype(F32), res[2 * i + 1, source].astype(F32)
             pair = jnp.where(left, swap(a), b) if high else jnp.where(left, a, swap(b))
             out_ref[t, :, 128 * i : 128 * i + 128] = pair.astype(BF16)
     last4 = (
         own4[...].T,
-        sum(res[m, 1].astype(F32) for m in range(4)),
+        swap(sum(res[m, 0].astype(F32) for m in range(4))),
         own,
         swap(own),
     )
@@ -528,37 +543,43 @@
     def block(dz):
         return lax.rem(z + dz + 8, 8)
 
-    def ship(dz, *names):
+    def ship(dz, way, i):
         u = block(dz)
-        for way in names:
-            sem, device = ways[way]
-            ref = gh.at[u, mine, :]
-            recv = (sib_r if way == "sib" else own_r).at[u]
-            if dz == -3 and way == "up":
-                ref, recv = gh.at[u, low, :], own_r.at[8]
-            if dz == 3 and way == "down":
-                ref, recv = gh.at[u, high, :], own_r.at[9]
-            sent.append(send(ref, ref, sem.at[count[way]], recv, device))
-            count[way] += 1
-
-    def arrive(dz, *names):
+        sem, device = ways[way]
+        if way == "sib":
+            ref, recv = gh.at[u, mine, :], sib_r.at[u]
+        else:
+            ref, recv = gh.at[u, (low, high)[i], :], own_r.at[2 * u + i]
+        sent.append(send(ref, ref, sem.at[count[way]], recv, device))
+        count[way] += 1
+
+    def arrive(dz):
         u = block(dz)
-        if dz == 4:
-            ref = gh.at[u, low, :]
-            remote(ref, ref, up_s.at[0], own_r.at[8], sib).wait_recv()
-            ref = gh.at[u, high, :]
-            remote(ref, ref, up_s.at[0], own_r.at[9], sib).wait_recv()
-        else:
-            ref = gh.at[u, mine, :]
-            remote(ref, ref, up_s.at[0], own_r.at[u], sib).wait_recv()
-        ship(dz, *names)
+        for i in range(2):
+            ref = gh.at[u, (low, high)[i], :]
+            remote(ref, ref, up_s.at[0], own_r.at[2 * u + i], sib).wait_recv()
+        ship(dz, "sib", 0)
+
+    def arrive_both(dz):
+        for i in range(2):
+            for d, way in ((-dz, "up"), (dz, "down")):
+                u = block(d)
+                ref = gh.at[u, (low, high)[i], :]
+                remote(ref, ref, up_s.at[0], own_r.at[2 * u + i], sib).wait_recv()
+                if dz < 3 or i == (0 if way == "up" else 1):
+                    ship(d, way, i)
+        ship(-dz, "sib", 0)
+        ship(dz, "sib", 0)
 
     edge = gh.at[z]
     near = [
         send(edge.at[high, :], halo.at[0], halo_s.at[0], halo_r.at[0], at_p(1)),
         send(edge.at[low, :], halo.at[1], halo_s.at[1], halo_r.at[1], at_p(-1)),
     ]
-    ship(0, "up", "down", "sib")
+    for i in range(2):
+        ship(0, "up", i)
+        ship(0, "down", i)
+    ship(0, "sib", 0)
 
     for i, t in enumerate((1, 2, 3, 0)):
         turned[...] = parts_ref[t].astype(F32).T.astype(BF16)
@@ -583,8 +604,7 @@
         theirs = pl.ds(pl.multiple_of((1 - core) * 640 + h * 320, 16), 320)
         there = pl.ds(320 * h, 320)
         pair.append(send(xs.at[theirs], half.at[there], pair_s.at[h], pair_r.at[h], sib))
-    arrive(-1, "up", "sib")
-    arrive(1, "down", "sib")
+    arrive_both(1)
 
     for copy in near:
         copy.wait()
@@ -634,8 +654,7 @@
         sent.append(send(half.at[low_of(0, h, far[h])], ra.at[h], y_s.at[h, 0], y_r.at[h, 0], up[h][1]))
         sent.append(send(half.at[high_of(0, h, far[h])], rb.at[h], y_s.at[h, 1], y_r.at[h, 1], down[h][1]))
     tap(1)
-    arrive(-2, "up", "sib")
-    arrive(2, "down", "sib")
+    arrive_both(2)
     for h in halves:
         remote(half.at[low_of(0, h, 0)], ra.at[h], y_s.at[h, 0], y_r.at[h, 0], sib).wait_recv()
         remote(half.at[high_of(0, h, 0)], rb.at[h], y_s.at[h, 1], y_r.at[h, 1], sib).wait_recv()
@@ -647,8 +666,7 @@
         sent.append(send(half.at[part(0, h, down[h][0])], rd.at[h], y_s.at[h, 3], y_r.at[h, 3], down[h][1]))
     tap(2)
     gain(0, True)
-    arrive(-3, "up", "sib")
-    arrive(3, "down", "sib")
+    arrive_both(3)
     gain(-1)
     def quarter(k):
         return pl.ds(pl.multiple_of(k * 128, 128), 128)
@@ -668,7 +686,7 @@
             other, device = second_at[h](s)
             crossing.append(send(plane.at[h, quarter(other)], xin.at[h, s], x_s.at[h, s], x_r.at[h, s], device))
     gain(1)
-    arrive(4, "sib")
+    arrive(4)
     for copy in crossing:
         copy.wait()
     for h in halves:
@@ -814,8 +832,8 @@
         f32(640, 128), b16(4, 640, 128), b16(4, 640, 128), b16(4, 640, 128), b16(4, 640, 128),
         f32(4, 72, 128), f32(4, 72, 128), f32(4, 8, 128), f32(128, 128), b16(3, 512, 128), b16(4, 3, 128, 128),
         dma((4,)), dma((4,)), dma((2, 4)), dma((2, 4)),
-        dma((4,)), dma((4,)), dma((4,)), dma((4,)), dma((4,)), dma((4,)), dma((4,)), dma((4,)),
-        dma((4,)), dma((4,)), dma((4,)), dma((4,)), dma((2, 4)), dma((2, 4)),
+        dma((4, 2)), dma((4, 2)), dma((4, 2)), dma((4, 2)), dma((4, 2)), dma((4, 2)), dma((4, 2)), dma((4, 2)),
+        dma((4,)), dma((4,)), dma((4,)), dma((4,)), dma((3, 4)), dma((3, 4)),
     ]
     three = [
         b16(8, 256, 640), b16(2, 64, 640), b16(3, 256, 640), f32(128, 640),
@@ -823,7 +841,7 @@
         b16(1280, 640), b16(640, 640), b16(2, 48, 640), b16(2, 32, 640), b16(2, 80, 640), b16(2, 80, 640),
         b16(2, 512, 128), b16(2, 4, 128, 128), b16(2, 128, 128), b16(8, 2, 16, 128), b16(2, 128, 128), b16(2, 512, 128),
         b16(2, 8, 128, 128), b16(16, 128, 128), b16(8, 128, 128),
-        dma((2,)), dma((2,)), dma((4,)), dma((4,)), dma((8,)), dma((10,)), dma((8,)),
+        dma((2,)), dma((2,)), dma((7,)), dma((7,)), dma((8,)), dma((16,)), dma((8,)),
         dma((2,)), dma((2,)), dma((2, 4)), dma((2, 4)), dma((2, 4)), dma((2, 4)), dma((8,)), dma((8,)),
         dma((8,)), dma((8,)), dma((2, 4)), dma((2, 4)), dma((2, 4)), dma((2, 4)), dma((2, 4)), dma((2, 4)),
         dma((16,)), dma((16,)), dma((8,)), dma((8,)),

time: 135 us -> 129 us (0.956)
  Pallas kernels: 133 us -> 128 us
    pallas_call x1, Pallas kernels: 130 us -> 125 us  [whole(): pl.pallas_call(whole_kernel, out_shape=(jax.ShapeDtypeStruct((1280, 640),...]
where the time goes in v4:
time: 129 us; the launch traced here: 128 us
  Pallas kernels  128 us (99%)
    pallas_call x1, Pallas kernels, whole(): pl.pallas_call(whole_kernel, out_shape=(jax.ShapeDtypeStruct((1280, 640),...  125 us
    pallas_call x1, Pallas kernels, hand_out(): pl.pallas_call(hand_kernel, out_shape=(jax.ShapeDtypeStruct(taps.shape, F...  3.09 us

profile of v4, /device:TPU:8, one launch (start us, length us, event | category | flops | bytes accessed | tf_op | source)
XLA Modules:
  0.0 128.5 jit_solution(431100908732290915)
XLA Ops:
  0.6 124.6 %whole.1 = (bf16[1280,640]{1,0:T(8,128)(2,1)}, f32[9,20,640]{2,1,0:T(8,128)}, bf16[128,640]{1,0:T(8,128)(2,1)}) custom-call(bf16[128,640]{1,0:T(8,128)(2,1)} %bitcast.15, bf16[128,640]{1,0:T(8,128)(2,1)} %bitcast.16, bf16[320,640]{1,0:T(8,128)(2,1)} %refs_2_.1, bf16[320,640]{1,0:T(8,128)(2,1)} %bitcast.12, bf16[320,640]{1,0:T(8,128)(2,1)} %bitcast.13, ...), custom_call_target="tpu_custom_call" | custom-call | tf_op jit(solution)/shard_map/whole/pallas_call | solution.py:849
  125.2 3.1 %hand_out.1 = (f32[9,20,640]{2,1,0:T(8,128)}, bf16[128,640]{1,0:T(8,128)(2,1)}, f32[320,640]{1,0:T(8,128)}, f32[320,640]{1,0:T(8,128)}, f32[320,640]{1,0:T(8,128)}, /*index=5*/f32[320,640]{1,0:T(8,128)}) custom-call(bf16[1280,640]{1,0:T(8,128)(2,1)} %get-tuple-element.15.rows_ref, f32[9,20,640]{2,1,0:T(8,128)} %get-tuple-element.16.taps_ref, ...), custom_call_target="tpu_custom_call" | custom-call | tf_op jit(solution)/shard_map/hand_out/pallas_call | solution.py:893

commit v5 on v4

--- a/solution.py
+++ b/solution.py
@@ -39,7 +39,7 @@
     )
 
 
-def attend_kernel(windows, lhs_ref, x_ref, out_ref, kv, kvt, qd, qs, gs, q4, g4, gt, gt4, scores, slope, pb, sb,
+def attend_kernel(windows, queries, lhs_ref, x_ref, out_ref, kv, kvt, qd, qs, gs, q4, g4, gt, gt4, scores, slope, pb, sb,
                   top, low, att, delta, dq, top4, low4, att4, delta4, dq4, part, box_up, box_down, ahead, behind,
                   mix, mix_in, stat, own4, stage, res,
                   kv_s, kv_r, qd_s, qd_r, up_s, up_r, down_s, down_r, rup_s, rup_r, rdown_s, rdown_r,
@@ -61,6 +61,7 @@
     for s in range(1, 4):
         m, device = in_quad(s)
         first.append(send(x_ref.at[2 * m], kv.at[z, rows(j), :], kv_s.at[s], kv_r.at[s], device))
+    queries()
     for s in range(1, 4):
         m, device = in_quad(s)
         second.append(send(x_ref.at[2 * m + 1], qd.at[0, rows(j), :], qd_s.at[0, s], qd_r.at[0, s], device))
@@ -172,24 +173,6 @@
     for s in range(1, 4):
         m, device = in_quad(s)
         late.append(send(stage.at[1, rows(m), :], res.at[j, 1], g_s.at[2, s], g_r.at[2, s], device))
-    for copy in mixing:
-        copy.wait()
-    tops = [mix_in[s, 64:65] for s in range(4)]
-    best = jnp.maximum(jnp.maximum(tops[0], tops[1]), jnp.maximum(tops[2], tops[3]))
-    total, blend = jnp.zeros((1, 128), F32), jnp.zeros((64, 128), F32)
-    for s in range(4):
-        weight = jnp.exp2(tops[s] - best)
-        total = total + mix_in[s, 65:66] * weight
-        blend = blend + mix_in[s, 0:64] * weight
-    blend = blend / total
-    own4[0:64] = blend
-    own4[64:128] = jnp.zeros((64, 128), F32)
-    stat[j, 0:1] = best + jnp.log2(total)
-    stat[j, 1:2] = jnp.sum(blend * gt4[:, rows(j)], axis=0, keepdims=True)
-    stat[j, 2:8] = jnp.zeros((6, 128), F32)
-    for s in range(1, 4):
-        stat_copy(s).start()
-
     def sum_up(s, i):
         return remote(box_up.at[s, cuts[i]], ahead.at[s, cuts[i]], rup_s.at[s, i], rup_r.at[s, i], at_z(1))
 
@@ -209,39 +192,73 @@
         pb[keys, q] = p.astype(BF16)
         sb[keys, q] = (p * (slope[keys, q] - delta[:, q])).astype(BF16)
 
+    def merge():
+        for copy in mixing:
+            copy.wait()
+        tops = [mix_in[s, 64:65] for s in range(4)]
+        best = jnp.maximum(jnp.maximum(tops[0], tops[1]), jnp.maximum(tops[2], tops[3]))
+        total, blend = jnp.zeros((1, 128), F32), jnp.zeros((64, 128), F32)
+        for s in range(4):
+            weight = jnp.exp2(tops[s] - best)
+            total = total + mix_in[s, 65:66] * weight
+            blend = blend + mix_in[s, 0:64] * weight
+        blend = blend / total
+        own4[0:64] = blend
+        own4[64:128] = jnp.zeros((64, 128), F32)
+        stat[j, 0:1] = best + jnp.log2(total)
+        stat[j, 1:2] = jnp.sum(blend * gt4[:, rows(j)], axis=0, keepdims=True)
+        stat[j, 2:8] = jnp.zeros((6, 128), F32)
+        for s in range(1, 4):
+            stat_copy(s).start()
+
+    def main_part(b):
+        slope[main] = lax.dot_general(kv[b, main], gs[...], NT, preferred_element_type=F32)
+        for q in quarters:
+            slopes(b, main, q, top, delta)
+        part[main] = jnp.dot(sb[main], qs[...], preferred_element_type=F32) + jnp.dot(
+            pb[main], gs[...], preferred_element_type=F32
+        )
+
+    def main_dq(b):
+        dq[...] += jnp.dot(kvt[b, 0:64, main], sb[main], preferred_element_type=F32)
+
+    def side_part(b):
+        slope[side] = lax.dot_general(kv[b, side], g4[...], NT, preferred_element_type=F32)
+        for q in quarters:
+            slopes(b, side, q, top4, delta4)
+        part[side] = jnp.dot(sb[side], q4[...], preferred_element_type=F32) + jnp.dot(
+            pb[side], g4[...], preferred_element_type=F32
+        )
+
+    def side_dq(b):
+        dq4[...] += jnp.dot(kvt[b, 0:64, side], sb[side], preferred_element_type=F32)
+
+    edge = lax.rem(z + 4, 8)
+    main_part(edge)
+    box_up[0, cuts[0]] = part[cuts[0]].astype(BF16)
+    sum_up(0, 0).start()
+    box_down[0, 320:512] = part[320:512].astype(BF16)
+    main_dq(edge)
+    merge()
+
     def pass_two(t, carry):
         offset = jnp.where(lax.rem(t, 2) == 0, 4 + t // 2, 4 - (t + 1) // 2)
         b = lax.rem(z + offset, 8)
-        slope[main] = lax.dot_general(kv[b, main], gs[...], NT, preferred_element_type=F32)
-        slope[side] = lax.dot_general(kv[b, side], g4[...], NT, preferred_element_type=F32)
-        for q in quarters:
-            slopes(b, main, q, top, delta)
-        dq[...] += jnp.dot(kvt[b, 0:64, main], sb[main], preferred_element_type=F32)
-        part[main] = jnp.dot(sb[main], qs[...], preferred_element_type=F32) + jnp.dot(
-            pb[main], gs[...], preferred_element_type=F32
-        )
-
-        @pl.when(t == 0)
+        main_part(b)
+
+        @pl.when(t == 1)
         def _():
             for s in range(1, 4):
                 stat_copy(s).wait()
             for m in range(4):
                 top4[:, quarters[m]] = stat[m, 0:1]
                 delta4[:, quarters[m]] = stat[m, 1:2]
-
-        for q in quarters:
-            slopes(b, side, q, top4, delta4)
-        dq4[...] += jnp.dot(kvt[b, 0:64, side], sb[side], preferred_element_type=F32)
-        part[side] = jnp.dot(sb[side], q4[...], preferred_element_type=F32) + jnp.dot(
-            pb[side], g4[...], preferred_element_type=F32
-        )
-
-        @pl.when(t == 0)
-        def _():
-            box_up[0, cuts[0]] = part[cuts[0]].astype(BF16)
-            sum_up(0, 0).start()
-            box_down[0, cuts[1]] = part[cuts[1]].astype(BF16)
+            side_part(edge)
+            box_down[0, side] = part[side].astype(BF16)
             sum_down(0, 1).start()
+            side_dq(edge)
+
+        side_part(b)
 
         @pl.when(t == 1)
         def _():
@@ -266,9 +283,11 @@
                 pass_on(box_down, behind, sum_down, s, 0)
                 pass_on(box_down, behind, sum_down, s, 1)
 
+        main_dq(b)
+        side_dq(b)
         return carry
 
-    lax.fori_loop(0, 8, pass_two, 0)
+    lax.fori_loop(1, 8, pass_two, 0)
     for q in quarters:
         both = jnp.concatenate([dq[:, q], dq4[:, q]], axis=0) * HD ** -0.5
         stage[0, q] = both.T.astype(BF16)
@@ -323,7 +342,7 @@
 
 
 def first_kernel(hbm, lat_ref, cot_ref, wq_ref, wk_ref, wv_ref, wo_ref, w, hid_ref, x_ref, load_sem, w_sem,
-                 halo, turned, sbuf, share, sh, acc, tmp, halo_s, halo_r, share_s, share_r, rim_s, rim_r):
+                 halo, turned, sbuf, share, sh, acc, tmp, kept, halo_s, halo_r, share_s, share_r, rim_s, rim_r):
     dp, xlo, z, core = place()
     p = lax.axis_index("patch")
     spot = dp * 2 + xlo
@@ -339,11 +358,9 @@
         copy = pltpu.make_async_copy(hbm[i], ref, load_sem.at[i])
         copy.start()
         inputs.append(copy)
-    loads = []
-    for t in range(9):
-        copy = pltpu.make_async_copy(hbm[6].at[t], w.at[t], w_sem.at[t])
-        copy.start()
-        loads.append(copy)
+    loads = [pltpu.make_async_copy(hbm[6].at[t], w.at[t], w_sem.at[t]) for t in range(9)]
+    for t in (3, 4, 5, 0, 1, 2, 6, 7, 8):
+        loads[t].start()
     barrier = pltpu.get_barrier_semaphore()
 
     def hello(s, carry):
@@ -416,27 +433,27 @@
     inputs[2].wait()
     out_grad = lax.dot_general(cot_ref[...], wo_ref[...], NT, preferred_element_type=F32)
     tmp[...] = jnp.zeros(tmp.shape, F32)
-    for copy in near:
-        copy.wait()
     j = lax.broadcasted_iota(jnp.int32, (64, 640), 0)
-    rows = (
-        jnp.where(p > 0, halo[0].astype(F32), 0.0),
-        lat_ref[0:64].astype(F32),
-        lat_ref[64:128].astype(F32),
-        jnp.where(p < 31, halo[1].astype(F32), 0.0),
-    )
-    for r in range(4):
-        moved = shifted(rows[r], j)
-        for b in range(3):
-            sh[b, 64 * r : 64 * r + 64] = moved[b].astype(BF16)
-    for t in range(9):
+
+    def lay(r, value):
+        for b, moved in enumerate(shifted(value, j)):
+            sh[b, 64 * r : 64 * r + 64] = moved.astype(BF16)
+
+    lay(1, lat_ref[0:64].astype(F32))
+    lay(2, lat_ref[64:128].astype(F32))
+    for t in (3, 4, 5, 0, 1, 2, 6, 7, 8):
         a, b = t // 3, t % 3
+        if t == 0:
+            for copy in near:
+                copy.wait()
+            lay(0, jnp.where(p > 0, halo[0].astype(F32), 0.0))
+            lay(3, jnp.where(p < 31, halo[1].astype(F32), 0.0))
         loads[t].wait()
         term = jnp.dot(sh[b, 64 * a : 64 * a + 128], w[t], preferred_element_type=F32)
-        if t:
+        if t == 3:
+            acc[...] = term
+        else:
             acc[...] += term
-        else:
-            acc[...] = term
     hid_ref[...] = acc[...].astype(BF16)
     for copy in inputs[3:]:
         copy.wait()
@@ -446,7 +463,10 @@
         return value.astype(BF16).astype(F32)
 
     pack(project(wk_ref), project(wv_ref), 0, 9)
-    pack(project(wq_ref) * HD ** -0.5, out_grad, 1, 8)
+    kept[...] = out_grad
+
+    def queries():
+        pack(project(wq_ref) * HD ** -0.5, kept[...], 1, 8)
 
     def windows(lhs_ref):
         def share_end(s, carry):
@@ -488,10 +508,10 @@
 
         lax.fori_loop(0, 16, one, 0)
 
-    return windows
-
-
-def finish_kernel(parts_ref, hid_ref, cot_ref, wq_ref, wk_ref, wv_ref, lhs_ref, w, out_ref, taps_ref, lat_ref,
+    return windows, queries
+
+
+def finish_kernel(parts_ref, both_ref, wq_ref, wk_ref, wv_ref, lhs_ref, w, out_ref, taps_ref, lat_ref,
                   gh, halo, sh, acc, prod, small, turned, xs, half, ra, rb, rc, rd,
                   plane, xin, xsum, zin, zfull, pfull, tb, tin, tfull, halo_s, halo_r, up_s, down_s, sib_s, own_r, sib_r,
                   pair_s, pair_r, y_s, y_r, x_s, x_r, z_s, z_r, zb_s, zb_r, xb_s, xb_r, yb_s, yb_r, fin_s, fin_r,
@@ -530,7 +550,7 @@
     mine = pl.ds(pl.multiple_of(core * 128, 128), 128)
     sent = []
 
-    value = cot_ref[...].astype(F32)
+    value = both_ref[1].astype(F32)
     for t, ref in ((1, wq_ref), (2, wk_ref), (3, wv_ref)):
         value = value + jnp.dot(parts_ref[t, :, 0:AW], ref[...], preferred_element_type=F32)
     gh[z, mine, :] = value.astype(BF16)
@@ -581,11 +601,6 @@
         ship(0, "down", i)
     ship(0, "sib", 0)
 
-    for i, t in enumerate((1, 2, 3, 0)):
-        turned[...] = parts_ref[t].astype(F32).T.astype(BF16)
-        right = hid_ref if t else cot_ref
-        xs[AW * i : AW * i + AW] = jnp.dot(turned[0:AW], right[...], preferred_element_type=F32).astype(BF16)
-
     first_at, second_at = (at_y, at_x), (at_x, at_y)
     first_index, second_index = (y, x), (x, y)
     halves = range(2)
@@ -600,10 +615,15 @@
         return pl.ds(pl.multiple_of(c * 640 + h * 320 + k * 80 + 48, 16), 32)
 
     pair = []
-    for h in halves:
-        theirs = pl.ds(pl.multiple_of((1 - core) * 640 + h * 320, 16), 320)
-        there = pl.ds(320 * h, 320)
-        pair.append(send(xs.at[theirs], half.at[there], pair_s.at[h], pair_r.at[h], sib))
+    for i in range(4):
+        k = lax.rem(2 * (1 - core) + i, 4)
+        t = lax.rem(k + 1, 4)
+        turned[...] = parts_ref[t].astype(F32).T.astype(BF16)
+        r = pl.ds(pl.multiple_of(k * AW, 16), AW)
+        right = both_ref[jnp.where(t == 0, 1, 0)]
+        xs[r] = jnp.dot(turned[0:AW], right, preferred_element_type=F32).astype(BF16)
+        if i < 2:
+            pair.append(send(xs.at[r], half.at[pl.ds(320 * i, 320)], pair_s.at[i], pair_r.at[i], sib))
     arrive_both(1)
 
     for copy in near:
@@ -796,12 +816,13 @@
 
 def whole_kernel(*refs):
     hbm, (rows_ref, taps_ref, lat_ref), scratch = refs[:7], refs[7:10], refs[10:]
-    shared, scratch = scratch[:11], scratch[11:]
-    latent, cot, wq, wk, wv, wo, w, hidden, packed, lhs, parts = shared
-    one, two, three = scratch[:15], scratch[15:15 + ATTEND], scratch[15 + ATTEND :]
-    windows = first_kernel(hbm, latent, cot, wq, wk, wv, wo, w, hidden, packed, *one)
-    attend_kernel(windows, lhs, packed, parts, *two)
-    finish_kernel(parts, hidden, cot, wq, wk, wv, lhs, w, rows_ref, taps_ref, lat_ref, *three)
+    shared, scratch = scratch[:10], scratch[10:]
+    latent, wq, wk, wv, wo, w, both, packed, lhs, parts = shared
+    hidden, cot = both.at[0], both.at[1]
+    one, two, three = scratch[:16], scratch[16 : 16 + ATTEND], scratch[16 + ATTEND :]
+    windows, queries = first_kernel(hbm, latent, cot, wq, wk, wv, wo, w, hidden, packed, *one)
+    attend_kernel(windows, queries, lhs, packed, parts, *two)
+    finish_kernel(parts, both, wq, wk, wv, lhs, w, rows_ref, taps_ref, lat_ref, *three)
 
 
 def whole(*args):
@@ -815,12 +836,12 @@
         return pltpu.VMEM(shape, F32)
 
     shared = [
-        b16(128, 640), b16(128, 640), b16(320, 640), b16(320, 640), b16(320, 640), b16(320, 640),
-        b16(9, 640, 640), b16(128, 640), b16(10, 128, 128), b16(8, 576, 256), b16(4, 128, 384),
+        b16(128, 640), b16(320, 640), b16(320, 640), b16(320, 640), b16(320, 640),
+        b16(9, 640, 640), b16(2, 128, 640), b16(10, 128, 128), b16(8, 576, 256), b16(4, 128, 384),
     ]
     one = [
         dma((6,)), dma((9,)), b16(2, 64, 640), f32(656, 128), b16(16, 2, 32, 128), b16(18, 2, 32, 128),
-        b16(3, 256, 640), f32(128, 640), f32(2, 128, 128),
+        b16(3, 256, 640), f32(128, 640), f32(2, 128, 128), f32(128, 320),
         dma((2,)), dma((2,)), dma((16,)), dma((16,)), dma((16,)), dma((1,)),
     ]
     two = [

time: 129 us -> 126 us (0.977)
  Pallas kernels: 128 us -> 125 us
    pallas_call x1, Pallas kernels: 125 us -> 122 us  [whole(): pl.pallas_call(whole_kernel, out_shape=(jax.ShapeDtypeStruct((1280, 640),...]
where the time goes in v5:
time: 126 us
  Pallas kernels  125 us (99%)
    pallas_call x1, Pallas kernels, whole(): pl.pallas_call(whole_kernel, out_shape=(jax.ShapeDtypeStruct((1280, 640),...  122 us
    pallas_call x1, Pallas kernels, hand_out(): pl.pallas_call(hand_kernel, out_shape=(jax.ShapeDtypeStruct(taps.shape, F...  3.09 us

profile of v5, /device:TPU:8, one launch (start us, length us, event | category | flops | bytes accessed | tf_op | source)
XLA Modules:
  0.0 125.7 jit_solution(15353661580948496439)
XLA Ops:
  0.6 121.8 %whole.1 = (bf16[1280,640]{1,0:T(8,128)(2,1)}, f32[9,20,640]{2,1,0:T(8,128)}, bf16[128,640]{1,0:T(8,128)(2,1)}) custom-call(bf16[128,640]{1,0:T(8,128)(2,1)} %bitcast.15, bf16[128,640]{1,0:T(8,128)(2,1)} %bitcast.16, bf16[320,640]{1,0:T(8,128)(2,1)} %refs_2_.1, bf16[320,640]{1,0:T(8,128)(2,1)} %bitcast.12, bf16[320,640]{1,0:T(8,128)(2,1)} %bitcast.13, ...), custom_call_target="tpu_custom_call" | custom-call | tf_op jit(solution)/shard_map/whole/pallas_call | solution.py:870
  122.4 3.1 %hand_out.1 = (f32[9,20,640]{2,1,0:T(8,128)}, bf16[128,640]{1,0:T(8,128)(2,1)}, f32[320,640]{1,0:T(8,128)}, f32[320,640]{1,0:T(8,128)}, f32[320,640]{1,0:T(8,128)}, /*index=5*/f32[320,640]{1,0:T(8,128)}) custom-call(bf16[1280,640]{1,0:T(8,128)(2,1)} %get-tuple-element.15.rows_ref, f32[9,20,640]{2,1,0:T(8,128)} %get-tuple-element.16.taps_ref, ...), custom_call_target="tpu_custom_call" | custom-call | tf_op jit(solution)/shard_map/hand_out/pallas_call | solution.py:914

commit v6 on v5

--- a/solution.py
+++ b/solution.py
@@ -707,6 +707,8 @@
             crossing.append(send(plane.at[h, quarter(other)], xin.at[h, s], x_s.at[h, s], x_r.at[h, s], device))
     gain(1)
     arrive(4)
+    gain(-2)
+    gain(2)
     for copy in crossing:
         copy.wait()
     for h in halves:
@@ -718,7 +720,9 @@
     for s in range(1, 8):
         other, device = at_z(s)
         along.append(send(xsum.at[:, slot(other), :], zin.at[s], z_s.at[s], z_r.at[s], device))
-    gain(-2)
+    gain(-3)
+    gain(3)
+    gain(4)
     whole = xsum[:, slot(z), :].astype(F32)
     for s in range(1, 8):
         along[s - 1].wait()
@@ -728,37 +732,6 @@
     for s in range(1, 8):
         ref = zfull.at[:, slot(z), :]
         zback.append(send(ref, ref, zb_s.at[s], zb_r.at[s], at_z(s)[1]))
-    gain(2)
-    for copy in zback:
-        copy.wait()
-    xback = []
-    for h in halves:
-        pfull[h, quarter(second_index[h])] = zfull[h]
-        for s in range(1, 4):
-            ref = pfull.at[h, quarter(second_index[h])]
-            xback.append(send(ref, ref, xb_s.at[h, s], xb_r.at[h, s], second_at[h](s)[1]))
-    gain(-3)
-    gain(3)
-    for copy in xback:
-        copy.wait()
-    fin = []
-    for h in halves:
-        for n in range(5):
-            out_ref[part(core, h, first_index[h]), 128 * n : 128 * n + 128] = pfull[h, 80 * n : 80 * n + 80]
-
-    def forward(rows, send_sem, recv_sem, device):
-        return send(out_ref.at[rows], out_ref.at[rows], send_sem, recv_sem, device)
-
-    def landed(rows, h, i):
-        remote(out_ref.at[rows], out_ref.at[rows], yb_s.at[h, i], yb_r.at[h, i], sib).wait_recv()
-
-    for h in halves:
-        rows = part(core, h, first_index[h])
-        sent.append(forward(rows, yb_s.at[h, 0], yb_r.at[h, 0], up[h][1]))
-        sent.append(forward(rows, yb_s.at[h, 1], yb_r.at[h, 1], down[h][1]))
-        fin.append(forward(rows, fin_s.at[h, 0], fin_r.at[h, 0], sib))
-    gain(4)
-
     places = [(n, i, 192 * n + 16 * i) for n in range(5) for i in range(12)]
     small[180:192] = jnp.zeros((12, 640), F32)
     for c in range(2):
@@ -772,7 +745,36 @@
     for s in range(1, 16):
         other, device = at_spot(s)
         there.append(send(tb.at[lax.rem(other, 2), other // 2], tin.at[s], t_s.at[s], t_r.at[s], device))
+    for copy in zback:
+        copy.wait()
+    xback = []
+    for h in halves:
+        pfull[h, quarter(second_index[h])] = zfull[h]
+        for s in range(1, 4):
+            ref = pfull.at[h, quarter(second_index[h])]
+            xback.append(send(ref, ref, xb_s.at[h, s], xb_r.at[h, s], second_at[h](s)[1]))
     tap(3)
+    tap(4)
+    for copy in xback:
+        copy.wait()
+    fin = []
+    for h in halves:
+        for n in range(5):
+            out_ref[part(core, h, first_index[h]), 128 * n : 128 * n + 128] = pfull[h, 80 * n : 80 * n + 80]
+
+    def forward(rows, send_sem, recv_sem, device):
+        return send(out_ref.at[rows], out_ref.at[rows], send_sem, recv_sem, device)
+
+    def landed(rows, h, i):
+        remote(out_ref.at[rows], out_ref.at[rows], yb_s.at[h, i], yb_r.at[h, i], sib).wait_recv()
+
+    for h in halves:
+        rows = part(core, h, first_index[h])
+        sent.append(forward(rows, yb_s.at[h, 0], yb_r.at[h, 0], up[h][1]))
+        sent.append(forward(rows, yb_s.at[h, 1], yb_r.at[h, 1], down[h][1]))
+        fin.append(forward(rows, fin_s.at[h, 0], fin_r.at[h, 0], sib))
+    tap(5)
+    tap(6)
     for h in halves:
         landed(part(core, h, down[h][0]), h, 0)
         landed(part(core, h, up[h][0]), h, 1)
@@ -780,13 +782,7 @@
         sent.append(forward(high_of(core, h, up[h][0]), yb_s.at[h, 3], yb_r.at[h, 3], down[h][1]))
         fin.append(forward(part(core, h, down[h][0]), fin_s.at[h, 1], fin_r.at[h, 1], sib))
         fin.append(forward(part(core, h, up[h][0]), fin_s.at[h, 2], fin_r.at[h, 2], sib))
-    tap(4)
-    tap(5)
-    for h in halves:
-        landed(low_of(core, h, far[h]), h, 2)
-        landed(high_of(core, h, far[h]), h, 3)
-        fin.append(forward(part(core, h, far[h]), fin_s.at[h, 3], fin_r.at[h, 3], sib))
-    tap(6)
+    tap(7)
     whole = tb[xlo, dp].astype(F32)
     for s in range(1, 16):
         there[s - 1].wait()
@@ -796,7 +792,10 @@
     for s in range(1, 8):
         ref = tfull.at[dp]
         tback.append(send(ref, ref, u_s.at[s], u_r.at[s], at_dp(s)[1]))
-    tap(7)
+    for h in halves:
+        landed(low_of(core, h, far[h]), h, 2)
+        landed(high_of(core, h, far[h]), h, 3)
+        fin.append(forward(part(core, h, far[h]), fin_s.at[h, 3], fin_r.at[h, 3], sib))
     tap(8)
     lat_ref[...] = acc[...].astype(BF16)
     for copy in tback:

time: 126 us -> 124 us (0.984)
  the two profiles are of different devices: /device:TPU:8 before, /device:TPU:1 now
where the time goes in v6:
time: 124 us
  Pallas kernels  123 us (99%)
    pallas_call x1, Pallas kernels, whole(): pl.pallas_call(whole_kernel, out_shape=(jax.ShapeDtypeStruct((1280, 640),...  120 us
    pallas_call x1, Pallas kernels, hand_out(): pl.pallas_call(hand_kernel, out_shape=(jax.ShapeDtypeStruct(taps.shape, F...  3.09 us

profile of v6, /device:TPU:1, one launch (start us, length us, event | category | flops | bytes accessed | tf_op | source)
XLA Modules:
  0.0 123.8 jit_solution(11014190279972455435)
XLA Ops:
  0.6 119.9 %whole.1 = (bf16[1280,640]{1,0:T(8,128)(2,1)}, f32[9,20,640]{2,1,0:T(8,128)}, bf16[128,640]{1,0:T(8,128)(2,1)}) custom-call(bf16[128,640]{1,0:T(8,128)(2,1)} %bitcast.15, bf16[128,640]{1,0:T(8,128)(2,1)} %bitcast.16, bf16[320,640]{1,0:T(8,128)(2,1)} %refs_2_.1, bf16[320,640]{1,0:T(8,128)(2,1)} %bitcast.12, bf16[320,640]{1,0:T(8,128)(2,1)} %bitcast.13, ...), custom_call_target="tpu_custom_call" | custom-call | tf_op jit(solution)/shard_map/whole/pallas_call | solution.py:869
  120.6 3.1 %hand_out.1 = (f32[9,20,640]{2,1,0:T(8,128)}, bf16[128,640]{1,0:T(8,128)(2,1)}, f32[320,640]{1,0:T(8,128)}, f32[320,640]{1,0:T(8,128)}, f32[320,640]{1,0:T(8,128)}, /*index=5*/f32[320,640]{1,0:T(8,128)}) custom-call(bf16[1280,640]{1,0:T(8,128)(2,1)} %get-tuple-element.15.rows_ref, f32[9,20,640]{2,1,0:T(8,128)} %get-tuple-element.16.taps_ref, ...), custom_call_target="tpu_custom_call" | custom-call | tf_op jit(solution)/shard_map/hand_out/pallas_call | solution.py:913

commit v7 on v6

--- a/solution.py
+++ b/solution.py
@@ -625,6 +625,17 @@
         if i < 2:
             pair.append(send(xs.at[r], half.at[pl.ds(320 * i, 320)], pair_s.at[i], pair_r.at[i], sib))
     arrive_both(1)
+    up, down, far = [], [], []
+    for h in halves:
+        up.append(first_at[h](1))
+        down.append(first_at[h](-1))
+        far.append(lax.rem(first_index[h] + 2, 4))
+        pair[h].wait()
+        mine_rows = pl.ds(pl.multiple_of(core * 640 + h * 320, 16), 320)
+        r = slice(320 * h, 320 * h + 320)
+        half[r] = (half[r].astype(F32) + xs[mine_rows].astype(F32)).astype(BF16)
+        sent.append(send(half.at[low_of(0, h, far[h])], ra.at[h], y_s.at[h, 0], y_r.at[h, 0], up[h][1]))
+        sent.append(send(half.at[high_of(0, h, far[h])], rb.at[h], y_s.at[h, 1], y_r.at[h, 1], down[h][1]))
 
     for copy in near:
         copy.wait()
@@ -660,20 +671,6 @@
             prod[...] += term
 
     tap(0)
-    for copy in pair:
-        copy.wait()
-    for h in halves:
-        mine_rows = pl.ds(pl.multiple_of(core * 640 + h * 320, 16), 320)
-        r = slice(320 * h, 320 * h + 320)
-        half[r] = (half[r].astype(F32) + xs[mine_rows].astype(F32)).astype(BF16)
-    up, down, far = [], [], []
-    for h in halves:
-        up.append(first_at[h](1))
-        down.append(first_at[h](-1))
-        far.append(lax.rem(first_index[h] + 2, 4))
-        sent.append(send(half.at[low_of(0, h, far[h])], ra.at[h], y_s.at[h, 0], y_r.at[h, 0], up[h][1]))
-        sent.append(send(half.at[high_of(0, h, far[h])], rb.at[h], y_s.at[h, 1], y_r.at[h, 1], down[h][1]))
-    tap(1)
     arrive_both(2)
     for h in halves:
         remote(half.at[low_of(0, h, 0)], ra.at[h], y_s.at[h, 0], y_r.at[h, 0], sib).wait_recv()
@@ -684,10 +681,10 @@
         half[r] = (half[r].astype(F32) + rb[h].astype(F32)).astype(BF16)
         sent.append(send(half.at[part(0, h, up[h][0])], rc.at[h], y_s.at[h, 2], y_r.at[h, 2], up[h][1]))
         sent.append(send(half.at[part(0, h, down[h][0])], rd.at[h], y_s.at[h, 3], y_r.at[h, 3], down[h][1]))
-    tap(2)
+    tap(1)
     gain(0, True)
     arrive_both(3)
-    gain(-1)
+    tap(2)
     def quarter(k):
         return pl.ds(pl.multiple_of(k * 128, 128), 128)
 
@@ -705,6 +702,7 @@
         for s in range(1, 4):
             other, device = second_at[h](s)
             crossing.append(send(plane.at[h, quarter(other)], xin.at[h, s], x_s.at[h, s], x_r.at[h, s], device))
+    gain(-1)
     gain(1)
     arrive(4)
     gain(-2)
@@ -885,20 +883,22 @@
 
 def hand_kernel(rows_ref, taps_ref, lat_ref, taps_out, lat_out, *rest):
     outs, (rows, wide, taps, lat, in_sem, out_sem) = rest[:4], rest[4:]
+    step = AW // 2
     loads = [
-        pltpu.make_async_copy(rows_ref.at[AW * i : AW * i + AW], rows.at[i], in_sem.at[i]) for i in range(4)
+        pltpu.make_async_copy(rows_ref.at[step * i : step * i + step], rows.at[i], in_sem.at[i]) for i in range(8)
     ]
-    loads.append(pltpu.make_async_copy(taps_ref, taps, in_sem.at[4]))
-    loads.append(pltpu.make_async_copy(lat_ref, lat, in_sem.at[5]))
+    loads.append(pltpu.make_async_copy(taps_ref, taps, in_sem.at[8]))
+    loads.append(pltpu.make_async_copy(lat_ref, lat, in_sem.at[9]))
     for copy in loads:
         copy.start()
     stores = []
-    for i in range(6):
+    for i in range(10):
         loads[i].wait()
-        if i < 4:
+        if i < 8:
             wide[i] = rows[i].astype(F32)
-            copy = pltpu.make_async_copy(wide.at[i], outs[i], out_sem.at[i])
-        elif i == 4:
+            place = outs[i // 2].at[step * (i % 2) : step * (i % 2) + step]
+            copy = pltpu.make_async_copy(wide.at[i], place, out_sem.at[i])
+        elif i == 8:
             copy = pltpu.make_async_copy(taps, taps_out, out_sem.at[i])
         else:
             copy = pltpu.make_async_copy(lat, lat_out, out_sem.at[i])
@@ -920,12 +920,12 @@
         in_specs=[anywhere] * 3,
         out_specs=(anywhere,) * 6,
         scratch_shapes=[
-            pltpu.VMEM((4, AW, 640), BF16),
-            pltpu.VMEM((4, AW, 640), F32),
+            pltpu.VMEM((8, AW // 2, 640), BF16),
+            pltpu.VMEM((8, AW // 2, 640), F32),
             pltpu.VMEM(taps.shape, F32),
             pltpu.VMEM(grad_latent.shape, BF16),
-            pltpu.SemaphoreType.DMA((6,)),
-            pltpu.SemaphoreType.DMA((6,)),
+            pltpu.SemaphoreType.DMA((10,)),
+            pltpu.SemaphoreType.DMA((10,)),
         ],
         compiler_params=pltpu.CompilerParams(vmem_limit_bytes=60 * 1024 * 1024),
         name="hand_out",

time: 124 us -> 123 us (level)
  the two profiles are of different devices: /device:TPU:1 before, /device:TPU:8 now
where the time goes in v7:
time: 123 us; the launch traced here: 121 us
  Pallas kernels  120 us (98%)
    pallas_call x1, Pallas kernels, whole(): pl.pallas_call(whole_kernel, out_shape=(jax.ShapeDtypeStruct((1280, 640),...  117 us
    pallas_call x1, Pallas kernels, hand_out(): pl.pallas_call(hand_kernel, out_shape=(jax.ShapeDtypeStruct(taps.shape, F...  3.06 us

profile of v7, /device:TPU:8, one launch (start us, length us, event | category | flops | bytes accessed | tf_op | source)
XLA Modules:
  0.0 120.6 jit_solution(15453851822199877892)
XLA Ops:
  0.6 116.7 %whole.1 = (bf16[1280,640]{1,0:T(8,128)(2,1)}, f32[9,20,640]{2,1,0:T(8,128)}, bf16[128,640]{1,0:T(8,128)(2,1)}) custom-call(bf16[128,640]{1,0:T(8,128)(2,1)} %bitcast.15, bf16[128,640]{1,0:T(8,128)(2,1)} %bitcast.16, bf16[320,640]{1,0:T(8,128)(2,1)} %refs_2_.1, bf16[320,640]{1,0:T(8,128)(2,1)} %bitcast.12, bf16[320,640]{1,0:T(8,128)(2,1)} %bitcast.13, ...), custom_call_target="tpu_custom_call" | custom-call | tf_op jit(solution)/shard_map/whole/pallas_call | solution.py:867
  117.4 3.1 %hand_out.1 = (f32[9,20,640]{2,1,0:T(8,128)}, bf16[128,640]{1,0:T(8,128)(2,1)}, f32[320,640]{1,0:T(8,128)}, f32[320,640]{1,0:T(8,128)}, f32[320,640]{1,0:T(8,128)}, /*index=5*/f32[320,640]{1,0:T(8,128)}) custom-call(bf16[1280,640]{1,0:T(8,128)(2,1)} %get-tuple-element.15.rows_ref, f32[9,20,640]{2,1,0:T(8,128)} %get-tuple-element.16.taps_ref, ...), custom_call_target="tpu_custom_call" | custom-call | tf_op jit(solution)/shard_map/hand_out/pallas_call | solution.py:913

commit v8 on v7

--- a/solution.py
+++ b/solution.py
@@ -511,7 +511,7 @@
     return windows, queries
 
 
-def finish_kernel(parts_ref, both_ref, wq_ref, wk_ref, wv_ref, lhs_ref, w, out_ref, taps_ref, lat_ref,
+def finish_kernel(rows_hbm, rows_sem, parts_ref, both_ref, wq_ref, wk_ref, wv_ref, lhs_ref, w, out_ref, taps_ref, lat_ref,
                   gh, halo, sh, acc, prod, small, turned, xs, half, ra, rb, rc, rd,
                   plane, xin, xsum, zin, zfull, pfull, tb, tin, tfull, halo_s, halo_r, up_s, down_s, sib_s, own_r, sib_r,
                   pair_s, pair_r, y_s, y_r, x_s, x_r, z_s, z_r, zb_s, zb_r, xb_s, xb_r, yb_s, yb_r, fin_s, fin_r,
@@ -794,18 +794,29 @@
         landed(low_of(core, h, far[h]), h, 2)
         landed(high_of(core, h, far[h]), h, 3)
         fin.append(forward(part(core, h, far[h]), fin_s.at[h, 3], fin_r.at[h, 3], sib))
+
+    def write(c, i):
+        r = pl.ds(pl.multiple_of(c * 640, 16), 640)
+        copy = pltpu.make_async_copy(out_ref.at[r], rows_hbm.at[r], rows_sem.at[i])
+        copy.start()
+        return copy
+
+    written = [write(core, 0)]
     tap(8)
     lat_ref[...] = acc[...].astype(BF16)
+    for copy in fin:
+        copy.wait()
+    written.append(write(1 - core, 1))
     for copy in tback:
         copy.wait()
     for n, i, f in places:
         small[16 * i : 16 * i + 16, 128 * n : 128 * n + 128] = tfull[f // 128, f % 128 : f % 128 + 16].astype(F32)
     for t in range(9):
         taps_ref[t] = small[20 * t : 20 * t + 20]
-    for copy in fin:
-        copy.wait()
     for copy in sent:
         copy.wait_send()
+    for copy in written:
+        copy.wait()
 
 
 ATTEND = 52
@@ -819,7 +830,8 @@
     one, two, three = scratch[:16], scratch[16 : 16 + ATTEND], scratch[16 + ATTEND :]
     windows, queries = first_kernel(hbm, latent, cot, wq, wk, wv, wo, w, hidden, packed, *one)
     attend_kernel(windows, queries, lhs, packed, parts, *two)
-    finish_kernel(parts, both, wq, wk, wv, lhs, w, rows_ref, taps_ref, lat_ref, *three)
+    rows_v, rows_sem, three = three[0], three[1], three[2:]
+    finish_kernel(rows_ref, rows_sem, parts, both, wq, wk, wv, lhs, w, rows_v, taps_ref, lat_ref, *three)
 
 
 def whole(*args):
@@ -854,6 +866,7 @@
         dma((4,)), dma((4,)), dma((4,)), dma((4,)), dma((3, 4)), dma((3, 4)),
     ]
     three = [
+        b16(1280, 640), dma((2,)),
         b16(8, 256, 640), b16(2, 64, 640), b16(3, 256, 640), f32(128, 640),
         f32(576, 640), f32(192, 640), b16(384, 128),
         b16(1280, 640), b16(640, 640), b16(2, 48, 640), b16(2, 32, 640), b16(2, 80, 640), b16(2, 80, 640),
@@ -872,7 +885,7 @@
             jax.ShapeDtypeStruct((128, 640), BF16),
         ),
         in_specs=[pl.BlockSpec(memory_space=pl.ANY)] * 7,
-        out_specs=(vmem,) * 3,
+        out_specs=(pl.BlockSpec(memory_space=pl.ANY), vmem, vmem),
         scratch_shapes=shared + one + two + three,
         compiler_params=pltpu.CompilerParams(
             collective_id=0, has_side_effects=True, vmem_limit_bytes=60 * 1024 * 1024

time: 123 us -> 123 us (level)
  the two profiles are of different devices: /device:TPU:8 before, /device:TPU:1 now
where the time goes in v8:
time: 123 us
  Pallas kernels  122 us (99%)
    pallas_call x1, Pallas kernels, whole(): pl.pallas_call(whole_kernel, out_shape=(jax.ShapeDtypeStruct((1280, 640),...  119 us
    pallas_call x1, Pallas kernels, hand_out(): pl.pallas_call(hand_kernel, out_shape=(jax.ShapeDtypeStruct(taps.shape, F...  3.06 us

profile of v8, /device:TPU:1, one launch (start us, length us, event | category | flops | bytes accessed | tf_op | source)
XLA Modules:
  0.0 123.2 jit_solution(17648609095755247009)
XLA Ops:
  0.6 119.3 %whole.1 = (bf16[1280,640]{1,0:T(8,128)(2,1)}, f32[9,20,640]{2,1,0:T(8,128)}, bf16[128,640]{1,0:T(8,128)(2,1)}) custom-call(bf16[128,640]{1,0:T(8,128)(2,1)} %bitcast.15, bf16[128,640]{1,0:T(8,128)(2,1)} %bitcast.16, bf16[320,640]{1,0:T(8,128)(2,1)} %refs_2_.1, bf16[320,640]{1,0:T(8,128)(2,1)} %bitcast.12, bf16[320,640]{1,0:T(8,128)(2,1)} %bitcast.13, ...), custom_call_target="tpu_custom_call" | custom-call | tf_op jit(solution)/shard_map/whole/pallas_call | solution.py:880
  120.0 3.1 %hand_out.1 = (f32[9,20,640]{2,1,0:T(8,128)}, bf16[128,640]{1,0:T(8,128)(2,1)}, f32[320,640]{1,0:T(8,128)}, f32[320,640]{1,0:T(8,128)}, f32[320,640]{1,0:T(8,128)}, /*index=5*/f32[320,640]{1,0:T(8,128)}) custom-call(bf16[1280,640]{1,0:T(8,128)(2,1)} %get-tuple-element.15.rows_ref, f32[9,20,640]{2,1,0:T(8,128)} %get-tuple-element.16.taps_ref, ...), custom_call_target="tpu_custom_call" | custom-call | tf_op jit(solution)/shard_map/hand_out/pallas_call | solution.py:926
